TPU v7x, 1024 devices: a whole 4x8x16 slice. The times are simulated.
1024 devices in a mesh: dp: 16 (over z), expert: 64 (over y, x, core).
Axes of the slice: x: 4, y: 8, z: 16, core: 2. Of those that a mesh axis runs over, the one named last changes fastest.
Arguments:
- activations: bfloat16 [2, 49152, 1024], P(None, ('dp', 'expert')), may hold values from -6 to 6
- out_grads: bfloat16 [2, 49152, 1024], P(None, ('dp', 'expert')), may hold values from -6 to 6
- chosen_ids: int32 [2, 16, 64, 96], P(None, 'dp', 'expert'), may hold values from 0 to 3071, as said below
- gate_logits: int32 [2, 16, 64, 96], P(None, 'dp', 'expert'), may hold values from -16384 to 16384
- w_gate: bfloat16 [64, 1024, 768], P('expert'), may hold values from -0.1875 to 0.1875
- w_up: bfloat16 [64, 1024, 768], P('expert'), may hold values from -0.1875 to 0.1875
- w_down: bfloat16 [64, 768, 1024], P('expert'), may hold values from -0.21875 to 0.21875
Outputs:
- token_grads: bfloat16 [2, 49152, 1024], P(None, ('dp', 'expert'))
- gate_wgrad: bfloat16 [64, 1024, 768], P('expert', 'dp')
- up_wgrad: bfloat16 [64, 1024, 768], P('expert', 'dp')
- down_wgrad: bfloat16 [64, 768, 1024], P('expert', 'dp')
Inputs may be any that keep to these rules, and one draw needn't show every extreme that they name: `chosen_ids`: each expert's 96 entries for one micro-batch and data group are distinct. At most 2 of them fall in one device's aligned block of 48 tokens, and in every list some block holds exactly 2.
All inputs are finite; a program needn't handle non-finite values.
Results may differ from a plain program's by a relative error of at most 0.023.
Values may be sent and summed in bfloat16 or wider, within the bound.
A program may use at most 32 MiB of HBM per device.

v0:
```python
import math

import jax
import jax.numpy as jnp
from jax import lax
from jax.sharding import PartitionSpec as P

contract_rows = (((0,), (0,)), ((), ()))
contract_cols = (((1,), (1,)), ((), ()))


def slot_layout(chosen, tok_dev, experts_n, slot_depth):
    holders = chosen // tok_dev
    inside = chosen - holders * tok_dev
    number = chosen.shape[0]
    before = lax.broadcasted_iota(jnp.int32, (number, number), 0) > lax.broadcasted_iota(
        jnp.int32, (number, number), 1
    )
    matches = holders[:, None] == holders[None, :]
    ranking = jnp.sum((matches & before).astype(jnp.int32), axis=1)
    places = holders * slot_depth + ranking
    wanted = jnp.full((experts_n * slot_depth,), -1, jnp.int32).at[places].set(inside)
    return (places, wanted.reshape(experts_n, slot_depth))


def pack_rows(tokens_here, grads_here, requested):
    keeper = (requested >= 0).astype(jnp.bfloat16)[..., None]
    safe_index = jnp.maximum(requested, 0)
    return (tokens_here[safe_index] * keeper, grads_here[safe_index] * keeper)


def collect(arrived, requested, tok_dev):
    flat_rows = arrived.reshape(-1, arrived.shape[-1])
    onehot = (
        requested.reshape(-1)[:, None] == lax.broadcasted_iota(jnp.int32, (1, tok_dev), 1)
    ).astype(jnp.bfloat16)
    return lax.dot_general(onehot, flat_rows, contract_rows, preferred_element_type=jnp.float32)


def expert_rows(got_x, got_g, places, logits, gate_mat, up_mat, down_mat, experts_n, slot_depth):
    width = got_x.shape[-1]
    picked_x = got_x.reshape(-1, width)[places]
    picked_g = got_g.reshape(-1, width)[places]
    gates = jax.nn.sigmoid(logits.astype(jnp.float32) * (1.0 / 4096.0))[:, None]
    hidden_gate = jnp.dot(picked_x, gate_mat, preferred_element_type=jnp.float32)
    hidden_up = jnp.dot(picked_x, up_mat, preferred_element_type=jnp.float32)
    sigma = jax.nn.sigmoid(hidden_gate)
    act_rows = (hidden_gate * sigma * hidden_up).astype(jnp.bfloat16)
    dy_rows = (gates * picked_g.astype(jnp.float32)).astype(jnp.bfloat16)
    dact = lax.dot_general(dy_rows, down_mat, contract_cols, preferred_element_type=jnp.float32)
    dh_up = (dact * hidden_gate * sigma).astype(jnp.bfloat16)
    dh_gate = (dact * hidden_up * sigma * (1.0 + hidden_gate * (1.0 - sigma))).astype(jnp.bfloat16)
    dx_rows = (
        lax.dot_general(dh_gate, gate_mat, contract_cols, preferred_element_type=jnp.float32)
        + lax.dot_general(dh_up, up_mat, contract_cols, preferred_element_type=jnp.float32)
    ).astype(jnp.bfloat16)
    outgoing = jnp.zeros((experts_n * slot_depth, width), jnp.bfloat16).at[places].set(dx_rows)
    return (
        outgoing.reshape(experts_n, slot_depth, width),
        (picked_x, act_rows, dy_rows, dh_gate, dh_up),
    )


def body(activations, out_grads, chosen_ids, gate_logits, w_gate, w_up, w_down):
    micros = activations.shape[0]
    tok_dev = activations.shape[1]
    experts_n = lax.axis_size("expert")
    groups_n = lax.axis_size("dp")
    capacity = chosen_ids.shape[-1]
    slot_depth = 3 * capacity // (2 * experts_n)
    gate_mat, up_mat, down_mat = (w_gate[0], w_up[0], w_down[0])
    layouts = [
        slot_layout(chosen_ids[index, 0, 0], tok_dev, experts_n, slot_depth)
        for index in range(micros)
    ]
    saved = []
    token_parts = []
    for index in range(micros):
        requested = lax.all_to_all(
            layouts[index][1], "expert", split_axis=0, concat_axis=0, tiled=True
        )
        rows_x, rows_g = pack_rows(activations[index], out_grads[index], requested)
        got_x, got_g = (
            lax.all_to_all(rows_x, "expert", split_axis=0, concat_axis=0, tiled=True),
            lax.all_to_all(rows_g, "expert", split_axis=0, concat_axis=0, tiled=True),
        )
        outgoing, kept = expert_rows(
            got_x,
            got_g,
            layouts[index][0],
            gate_logits[index, 0, 0],
            gate_mat,
            up_mat,
            down_mat,
            experts_n,
            slot_depth,
        )
        saved.append(kept)
        arrived = lax.all_to_all(outgoing, "expert", split_axis=0, concat_axis=0, tiled=True)
        token_parts.append(collect(arrived, requested, tok_dev))
    token_grads = jnp.stack(token_parts).astype(jnp.bfloat16)
    inputs_all = jnp.concatenate([item[0] for item in saved], axis=0)
    act_all = jnp.concatenate([item[1] for item in saved], axis=0)
    dy_all = jnp.concatenate([item[2] for item in saved], axis=0)
    dgate_all = jnp.concatenate([item[3] for item in saved], axis=0)
    dup_all = jnp.concatenate([item[4] for item in saved], axis=0)
    factor = 1.0 / math.sqrt(groups_n * micros * capacity)

    def outer(left, right):
        return (
            lax.dot_general(left, right, contract_rows, preferred_element_type=jnp.float32) * factor
        )

    gate_sum, up_sum, down_sum = (
        lax.psum_scatter(
            outer(inputs_all, dgate_all)[None].astype(jnp.bfloat16),
            "dp",
            scatter_dimension=1,
            tiled=True,
        ).astype(jnp.float32),
        lax.psum_scatter(
            outer(inputs_all, dup_all)[None].astype(jnp.bfloat16),
            "dp",
            scatter_dimension=1,
            tiled=True,
        ).astype(jnp.float32),
        lax.psum_scatter(
            outer(act_all, dy_all)[None].astype(jnp.bfloat16), "dp", scatter_dimension=1, tiled=True
        ).astype(jnp.float32),
    )
    gate_wgrad = gate_sum.astype(jnp.bfloat16)
    up_wgrad = up_sum.astype(jnp.bfloat16)
    down_wgrad = down_sum.astype(jnp.bfloat16)
    return (token_grads, gate_wgrad, up_wgrad, down_wgrad)


def solution(mesh):
    placed = (
        P(None, ("dp", "expert"), None),
        P(None, ("dp", "expert"), None),
        P(None, "dp", "expert", None),
        P(None, "dp", "expert", None),
        P("expert", None, None),
        P("expert", None, None),
        P("expert", None, None),
    )
    return jax.shard_map(
        body,
        mesh=mesh,
        in_specs=placed,
        out_specs=(
            P(None, ("dp", "expert"), None),
            P("expert", "dp", None),
            P("expert", "dp", None),
            P("expert", "dp", None),
        ),
        check_vma=False,
    )
```

profile of v0, /device:TPU:2, one launch (start us, length us, event | category | flops | bytes accessed | tf_op | source)
XLA Modules:
  0.0 367.1 jit_solution(13374728150485428300)
XLA Ops:
  7.2 0.8 bitcast_subtract_fusion.1
  8.2 0.7 fusion.59
  8.9 0.9 scatter_custom_fusion
  9.8 0.8 all_to_all.30
  10.5 17.2 %all-to-all-start = ((s32[64,1,2]{2,1,0:T(1,128)}), s32[64,1,2]{2,1,0:T(1,128)S(1)}, u32[]{:S(2)}, u32[]{:S(2)}) async-start(s32[64,1,2]{2,1,0:T(1,128)} %bitcast.5), calls=%async_computation | async-start | bytes 65536 | tf_op jit(solution)/shard_map/all_to_all | solution.py:79
  27.7 1.0 slice_bitcast_fusion.3
  28.7 1.0 slice_bitcast_fusion.2
  29.6 0.9 scatter_custom_fusion.2
  30.5 0.8 all_to_all.35
  31.3 5.1 %all-to-all-done = s32[64,1,2]{2,1,0:T(1,128)S(1)} async-done(((s32[64,1,2]{2,1,0:T(1,128)}), s32[64,1,2]{2,1,0:T(1,128)S(1)}, u32[]{:S(2)}, u32[]{:S(2)}) %all-to-all-start) | async-done | bytes 544 | tf_op jit(solution)/shard_map/all_to_all | solution.py:79
  36.3 5.5 %all-to-all-start.4 = ((s32[64,1,2]{2,1,0:T(1,128)}), s32[64,1,2]{2,1,0:T(1,128)S(1)}, u32[]{:S(2)}, u32[]{:S(2)}) async-start(s32[64,1,2]{2,1,0:T(1,128)} %bitcast.19), calls=%async_computation.4 | async-start | bytes 65536 | tf_op jit(solution)/shard_map/all_to_all | solution.py:79
  42.2 0.9 gather_fusion
  43.2 0.9 gather_fusion.2
  44.2 1.4 broadcast_multiply_fusion.3
  45.6 4.9 %all-to-all-done.4 = s32[64,1,2]{2,1,0:T(1,128)S(1)} async-done(((s32[64,1,2]{2,1,0:T(1,128)}), s32[64,1,2]{2,1,0:T(1,128)S(1)}, u32[]{:S(2)}, u32[]{:S(2)}) %all-to-all-start.4) | async-done | bytes 544 | tf_op jit(solution)/shard_map/all_to_all | solution.py:79
  50.5 5.5 %all-to-all-start.1 = ((bf16[64,2,1024]{2,1,0:T(2,128)(2,1)}), bf16[64,2,1024]{2,1,0:T(2,128)(2,1)S(1)}, u32[]{:S(2)}, u32[]{:S(2)}) async-start(bf16[64,2,1024]{2,1,0:T(2,128)(2,1)} %get-tuple-element.18), calls=%async_computation.1 | async-start | bytes 524288 | tf_op jit(solution)/shard_map/all_to_all | solution.py:85
  56.4 11.9 %all-to-all-done.1 = bf16[64,2,1024]{2,1,0:T(2,128)(2,1)S(1)} async-done(((bf16[64,2,1024]{2,1,0:T(2,128)(2,1)}), bf16[64,2,1024]{2,1,0:T(2,128)(2,1)S(1)}, u32[]{:S(2)}, u32[]{:S(2)}) %all-to-all-start.1) | async-done | bytes 262176 | tf_op jit(solution)/shard_map/all_to_all | solution.py:85
  68.3 0.7 copy-done.6
  69.0 5.7 %all-to-all-start.2 = ((bf16[64,2,1024]{2,1,0:T(2,128)(2,1)}), bf16[64,2,1024]{2,1,0:T(2,128)(2,1)S(1)}, u32[]{:S(2)}, u32[]{:S(2)}) async-start(bf16[64,2,1024]{2,1,0:T(2,128)(2,1)} %get-tuple-element.19), calls=%async_computation.2 | async-start | bytes 524288 | tf_op jit(solution)/shard_map/all_to_all | solution.py:84
  74.7 0.9 gather_fusion.6
  75.7 0.9 gather_fusion.4
  76.8 1.4 broadcast_multiply_fusion.1
  78.1 8.8 %all-to-all-done.2 = bf16[64,2,1024]{2,1,0:T(2,128)(2,1)S(1)} async-done(((bf16[64,2,1024]{2,1,0:T(2,128)(2,1)}), bf16[64,2,1024]{2,1,0:T(2,128)(2,1)S(1)}, u32[]{:S(2)}, u32[]{:S(2)}) %all-to-all-start.2) | async-done | bytes 262176 | tf_op jit(solution)/shard_map/all_to_all | solution.py:84
  86.9 6.0 %all-to-all-start.5 = ((bf16[64,2,1024]{2,1,0:T(2,128)(2,1)}), bf16[64,2,1024]{2,1,0:T(2,128)(2,1)}, u32[]{:S(2)}, u32[]{:S(2)}) async-start(bf16[64,2,1024]{2,1,0:T(2,128)(2,1)} %get-tuple-element.20), calls=%async_computation.5 | async-start | bytes 524288 | tf_op jit(solution)/shard_map/all_to_all | solution.py:85
  93.0 1.2 reshape.315
  94.2 1.5 gather_fusion.1
  95.6 1.0 multiply_convert_fusion.4
  96.7 8.5 %all-to-all-done.5 = bf16[64,2,1024]{2,1,0:T(2,128)(2,1)} async-done(((bf16[64,2,1024]{2,1,0:T(2,128)(2,1)}), bf16[64,2,1024]{2,1,0:T(2,128)(2,1)}, u32[]{:S(2)}, u32[]{:S(2)}) %all-to-all-start.5) | async-done | bytes 262176 | tf_op jit(solution)/shard_map/all_to_all | solution.py:85
  105.2 6.1 %all-to-all-start.6 = ((bf16[64,2,1024]{2,1,0:T(2,128)(2,1)}), bf16[64,2,1024]{2,1,0:T(2,128)(2,1)}, u32[]{:S(2)}, u32[]{:S(2)}) async-start(bf16[64,2,1024]{2,1,0:T(2,128)(2,1)} %get-tuple-element.21), calls=%async_computation.6 | async-start | bytes 524288 | tf_op jit(solution)/shard_map/all_to_all | solution.py:84
  111.5 1.3 fusion.18
  112.8 1.0 reshape.316
  113.9 1.5 gather_fusion.3
  115.3 1.0 reshape.319
  116.4 1.5 gather_fusion.5
  117.9 1.0 multiply_convert_fusion.3
  118.9 0.7 copy-done.9
  119.6 1.3 fusion.16
  120.9 2.6 all-to-all-done.6
  123.5 1.0 reshape.320
  124.5 1.5 gather_fusion.7
  126.0 1.4 fusion.6
  127.8 1.2 multiply_convert_fusion.6
  129.0 1.2 multiply_convert_fusion.5
  130.2 1.8 fusion.22
  132.1 0.7 copy-done.21
  132.8 2.8 fusion.21
  135.8 2.8 fusion.20
  139.4 1.3 fusion.32
  140.7 1.5 scatter_custom_fusion.1
  142.2 0.8 reshape.317
  143.0 8.0 %all-to-all-start.3 = ((bf16[64,2,1024]{2,1,0:T(2,128)(2,1)}), bf16[64,2,1024]{2,1,0:T(2,128)(2,1)S(1)}, u32[]{:S(2)}, u32[]{:S(2)}) async-start(bf16[64,2,1024]{2,1,0:T(2,128)(2,1)} %reshape.317), calls=%async_computation.3 | async-start | bytes 524288 | tf_op jit(solution)/shard_map/all_to_all | solution.py:99
  151.0 1.5 fusion
  152.5 0.6 fusion.29
  153.1 1.2 scatter_custom_fusion.3
  154.3 0.8 reshape.321
  155.2 8.0 %all-to-all-done.3 = bf16[64,2,1024]{2,1,0:T(2,128)(2,1)S(1)} async-done(((bf16[64,2,1024]{2,1,0:T(2,128)(2,1)}), bf16[64,2,1024]{2,1,0:T(2,128)(2,1)S(1)}, u32[]{:S(2)}, u32[]{:S(2)}) %all-to-all-start.3) | async-done | bytes 262176 | tf_op jit(solution)/shard_map/all_to_all | solution.py:99
  163.2 5.7 %all-to-all-start.7 = ((bf16[64,2,1024]{2,1,0:T(2,128)(2,1)}), bf16[64,2,1024]{2,1,0:T(2,128)(2,1)S(1)}, u32[]{:S(2)}, u32[]{:S(2)}) async-start(bf16[64,2,1024]{2,1,0:T(2,128)(2,1)} %reshape.321), calls=%async_computation.7 | async-start | bytes 524288 | tf_op jit(solution)/shard_map/all_to_all | solution.py:99
  169.4 0.7 reduce.7
  170.2 0.7 reduce.6
  171.2 9.8 %all-to-all-done.7 = bf16[64,2,1024]{2,1,0:T(2,128)(2,1)S(1)} async-done(((bf16[64,2,1024]{2,1,0:T(2,128)(2,1)}), bf16[64,2,1024]{2,1,0:T(2,128)(2,1)S(1)}, u32[]{:S(2)}, u32[]{:S(2)}) %all-to-all-start.7) | async-done | bytes 262176 | tf_op jit(solution)/shard_map/all_to_all | solution.py:99
  181.8 0.7 pad_maximum_fusion
  182.5 23.9 %reduce-scatter.8.cloned.1.call-done = bf16[1,48,1024]{2,1,0:T(8,128)(2,1)} async-done(((bf16[1,768,1024]{2,1,0:T(8,128)(2,1)}), bf16[1,48,1024]{2,1,0:T(8,128)(2,1)}) %reduce-scatter.8.cloned.1.call-update) | async-done | bytes 98320 | tf_op jit(solution)/shard_map/reduce_scatter | solution.py:127
  206.3 77.5 %reduce-scatter.6.cloned.1.call-done = bf16[1,64,768]{2,1,0:T(8,128)(2,1)} async-done(((bf16[1,1024,768]{2,1,0:T(8,128)(2,1)}), bf16[1,64,768]{2,1,0:T(8,128)(2,1)}) %reduce-scatter.6.cloned.1.call-update) | async-done | bytes 98320 | tf_op jit(solution)/shard_map/reduce_scatter | solution.py:121
  283.8 76.8 %reduce-scatter.4.cloned.1.call-done = bf16[1,64,768]{2,1,0:T(8,128)(2,1)} async-done(((bf16[1,1024,768]{2,1,0:T(8,128)(2,1)}), bf16[1,64,768]{2,1,0:T(8,128)(2,1)}) %reduce-scatter.4.cloned.1.call-update) | async-done | bytes 98320 | tf_op jit(solution)/shard_map/reduce_scatter | solution.py:115
  (84 shorter events, 4.8 us)
Async XLA Ops:
  7.2 120.6 %copy-start = (bf16[1,1024,768]{2,1,0:T(8,128)(2,1)S(1)}, bf16[1,1024,768]{2,1,0:T(8,128)(2,1)}, u32[]{:S(2)}) copy-start(bf16[1,1024,768]{2,1,0:T(8,128)(2,1)} %param.12) | copy-start | bytes 4718596
  8.9 84.1 %copy-start.22 = (s32[96]{0:T(128)}, s32[96]{0:T(128)S(1)}, u32[]{:S(2)}) copy-start(s32[96]{0:T(128)S(1)} %get-tuple-element.25) | copy-start | bytes 1156
  10.5 25.8 %all-to-all-start = ((s32[64,1,2]{2,1,0:T(1,128)}), s32[64,1,2]{2,1,0:T(1,128)S(1)}, u32[]{:S(2)}, u32[]{:S(2)}) async-start(s32[64,1,2]{2,1,0:T(1,128)} %bitcast.5), calls=%async_computation | async-start | bytes 65536 | tf_op jit(solution)/shard_map/all_to_all | solution.py:79
  36.3 5.7 %copy-start.11 = (s32[64,1,2]{2,1,0:T(1,128)}, s32[64,1,2]{2,1,0:T(1,128)S(1)}, u32[]{:S(2)}) copy-start(s32[64,1,2]{2,1,0:T(1,128)S(1)} %all-to-all-done) | copy-start | bytes 1540
  36.3 14.1 %all-to-all-start.4 = ((s32[64,1,2]{2,1,0:T(1,128)}), s32[64,1,2]{2,1,0:T(1,128)S(1)}, u32[]{:S(2)}, u32[]{:S(2)}) async-start(s32[64,1,2]{2,1,0:T(1,128)} %bitcast.19), calls=%async_computation.4 | async-start | bytes 65536 | tf_op jit(solution)/shard_map/all_to_all | solution.py:79
  50.5 25.1 %copy-start.13 = (s32[64,1,2]{2,1,0:T(1,128)}, s32[64,1,2]{2,1,0:T(1,128)S(1)}, u32[]{:S(2)}) copy-start(s32[64,1,2]{2,1,0:T(1,128)S(1)} %all-to-all-done.4) | copy-start | bytes 1540
  50.5 17.8 %all-to-all-start.1 = ((bf16[64,2,1024]{2,1,0:T(2,128)(2,1)}), bf16[64,2,1024]{2,1,0:T(2,128)(2,1)S(1)}, u32[]{:S(2)}, u32[]{:S(2)}) async-start(bf16[64,2,1024]{2,1,0:T(2,128)(2,1)} %get-tuple-element.18), calls=%async_computation.1 | async-start | bytes 524288 | tf_op jit(solution)/shard_map/all_to_all | solution.py:85
  68.3 0.7 copy-start.6
  69.0 17.9 %all-to-all-start.2 = ((bf16[64,2,1024]{2,1,0:T(2,128)(2,1)}), bf16[64,2,1024]{2,1,0:T(2,128)(2,1)S(1)}, u32[]{:S(2)}, u32[]{:S(2)}) async-start(bf16[64,2,1024]{2,1,0:T(2,128)(2,1)} %get-tuple-element.19), calls=%async_computation.2 | async-start | bytes 524288 | tf_op jit(solution)/shard_map/all_to_all | solution.py:84
  76.5 16.4 %copy-start.23 = (s32[2,1,1,96]{3,2,1,0:T(1,128)S(1)}, s32[2,1,1,96]{3,2,1,0:T(1,128)}, u32[]{:S(2)}) copy-start(s32[2,1,1,96]{3,2,1,0:T(1,128)} %param.10) | copy-start | bytes 2308
  86.9 6.1 %copy-start.5 = (bf16[64,2,1024]{2,1,0:T(2,128)(2,1)}, bf16[64,2,1024]{2,1,0:T(2,128)(2,1)S(1)}, u32[]{:S(2)}) copy-start(bf16[64,2,1024]{2,1,0:T(2,128)(2,1)S(1)} %all-to-all-done.2) | copy-start | bytes 786436
  86.9 18.3 %all-to-all-start.5 = ((bf16[64,2,1024]{2,1,0:T(2,128)(2,1)}), bf16[64,2,1024]{2,1,0:T(2,128)(2,1)}, u32[]{:S(2)}, u32[]{:S(2)}) async-start(bf16[64,2,1024]{2,1,0:T(2,128)(2,1)} %get-tuple-element.20), calls=%async_computation.5 | async-start | bytes 524288 | tf_op jit(solution)/shard_map/all_to_all | solution.py:85
  93.0 18.5 %copy-start.2 = (bf16[1,768,1024]{2,1,0:T(8,128)(2,1)S(1)}, bf16[1,768,1024]{2,1,0:T(8,128)(2,1)}, u32[]{:S(2)}) copy-start(bf16[1,768,1024]{2,1,0:T(8,128)(2,1)} %param.13) | copy-start | bytes 4718596
  96.7 14.8 %copy-start.7 = (bf16[96,1024]{1,0:T(8,128)(2,1)}, bf16[96,1024]{1,0:T(8,128)(2,1)S(1)}, u32[]{:S(2)}) copy-start(bf16[96,1024]{1,0:T(8,128)(2,1)S(1)} %multiply_convert_fusion.4) | copy-start | bytes 589828
  105.2 18.3 %all-to-all-start.6 = ((bf16[64,2,1024]{2,1,0:T(2,128)(2,1)}), bf16[64,2,1024]{2,1,0:T(2,128)(2,1)}, u32[]{:S(2)}, u32[]{:S(2)}) async-start(bf16[64,2,1024]{2,1,0:T(2,128)(2,1)} %get-tuple-element.21), calls=%async_computation.6 | async-start | bytes 524288 | tf_op jit(solution)/shard_map/all_to_all | solution.py:84
  111.2 95.1 %reduce-scatter.8.cloned.1.call-start = ((), (), s32[]{:S(2)}) async-start(), calls=%async_computation.13 | async-start | bytes 1671168 | tf_op jit(solution)/shard_map/reduce_scatter | solution.py:127
  118.9 0.7 copy-start.9
  120.9 5.1 %copy-start.1 = (bf16[1,1024,768]{2,1,0:T(8,128)(2,1)S(1)}, bf16[1,1024,768]{2,1,0:T(8,128)(2,1)}, u32[]{:S(2)}) copy-start(bf16[1,1024,768]{2,1,0:T(8,128)(2,1)} %param.11) | copy-start | bytes 4718596
  126.0 1.4 copy-start.4
  126.0 1.8 copy-start.3
  126.0 1.8 copy-start.15
  127.8 1.2 copy-start.16
  129.0 1.2 copy-start.8
  129.0 1.2 copy-start.10
  132.0 151.8 %reduce-scatter.6.cloned.1.call-start = ((), (), s32[]{:S(2)}) async-start(), calls=%async_computation.12 | async-start | bytes 1671168 | tf_op jit(solution)/shard_map/reduce_scatter | solution.py:121
  132.1 0.7 copy-start.21
  132.8 2.9 copy-start.18
  132.8 2.9 copy-start.20
  135.7 224.9 %reduce-scatter.4.cloned.1.call-start = ((), (), s32[]{:S(2)}) async-start(), calls=%async_computation.11 | async-start | bytes 1671168 | tf_op jit(solution)/shard_map/reduce_scatter | solution.py:115
  138.5 0.9 copy-start.19
  142.2 10.3 %copy-start.17 = (bf16[96,768]{1,0:T(8,128)(2,1)S(1)}, bf16[96,768]{1,0:T(8,128)(2,1)}, u32[]{:S(2)}) copy-start(bf16[96,768]{1,0:T(8,128)(2,1)} %get-tuple-element.13) | copy-start | bytes 442372
  143.0 20.2 %all-to-all-start.3 = ((bf16[64,2,1024]{2,1,0:T(2,128)(2,1)}), bf16[64,2,1024]{2,1,0:T(2,128)(2,1)S(1)}, u32[]{:S(2)}, u32[]{:S(2)}) async-start(bf16[64,2,1024]{2,1,0:T(2,128)(2,1)} %reshape.317), calls=%async_computation.3 | async-start | bytes 524288 | tf_op jit(solution)/shard_map/all_to_all | solution.py:99
  152.5 16.9 %copy-start.12 = (s32[64,1,2]{2,1,0:T(1,128)S(1)}, s32[64,1,2]{2,1,0:T(1,128)}, u32[]{:S(2)}) copy-start(s32[64,1,2]{2,1,0:T(1,128)} %copy-done.11) | copy-start | bytes 1540
  152.5 17.7 %copy-start.14 = (s32[64,1,2]{2,1,0:T(1,128)S(1)}, s32[64,1,2]{2,1,0:T(1,128)}, u32[]{:S(2)}) copy-start(s32[64,1,2]{2,1,0:T(1,128)} %copy-done.13) | copy-start | bytes 1540
  163.2 17.9 %all-to-all-start.7 = ((bf16[64,2,1024]{2,1,0:T(2,128)(2,1)}), bf16[64,2,1024]{2,1,0:T(2,128)(2,1)S(1)}, u32[]{:S(2)}, u32[]{:S(2)}) async-start(bf16[64,2,1024]{2,1,0:T(2,128)(2,1)} %reshape.321), calls=%async_computation.7 | async-start | bytes 524288 | tf_op jit(solution)/shard_map/all_to_all | solution.py:99
Sparse Core Ops, SparseCore 0:
  132.1 74.1 reduce-scatter.7
  210.7 73.0 reduce-scatter.5
  287.8 72.7 reduce-scatter.3
where the time goes:
time: 368 us; the launch traced here: 367 us
  waiting for transfers between devices  238 us (65%)
  starting transfers between devices  59.9 us (16%)
  local copies, waits for them, and re-layouts  27.9 us (8%)
  matrix products  18.7 us (5%)
  between operations  14.3 us (4%)
  other arithmetic  8.67 us (2%)
    reduce_scatter x1, waiting for transfers between devices, body(): lax.psum_scatter(outer(inputs_all, dup_all)[None].astype(jnp.bfloat16), '...  77.5 us
    reduce_scatter x1, waiting for transfers between devices, body(): lax.psum_scatter(outer(inputs_all, dgate_all)[None].astype(jnp.bfloat16),...  76.8 us
    reduce_scatter x1, waiting for transfers between devices, body(): lax.psum_scatter(outer(act_all, dy_all)[None].astype(jnp.bfloat16), 'dp',...  23.9 us
    all_to_all x2, starting transfers between devices, body(): lax.all_to_all(layouts[index][1], 'expert', split_axis=0, concat_axis=0,...  22.7 us
    all_to_all x2, waiting for transfers between devices, body(): lax.all_to_all(rows_g, 'expert', split_axis=0, concat_axis=0, tiled=True)  20.4 us
    all_to_all x2, waiting for transfers between devices, body(): lax.all_to_all(outgoing, 'expert', split_axis=0, concat_axis=0, tiled=True)  17.9 us
    all_to_all x2, starting transfers between devices, body(): lax.all_to_all(outgoing, 'expert', split_axis=0, concat_axis=0, tiled=True)  13.6 us
    all_to_all x2, starting transfers between devices, body(): lax.all_to_all(rows_x, 'expert', split_axis=0, concat_axis=0, tiled=True)  11.7 us
  transfers between devices with their start and end apart: 11, of which 11 were waited for; matrix products, arithmetic and copies ran while one was open for 11% of the time, Pallas kernels for 0%

commit v1 on v0

v1 whole, which is shorter than its diff:
```python
import functools
import math

import jax
import jax.numpy as jnp
from jax import lax
from jax.experimental import pallas as pl
from jax.experimental.pallas import tpu as pltpu
from jax.sharding import PartitionSpec as P

MESH = pl.DeviceIdType.MESH
BF16 = jnp.bfloat16
F32 = jnp.float32
contract_rows = (((0,), (0,)), ((), ()))
contract_cols = (((1,), (1,)), ((), ()))


def iota(shape, axis):
    return lax.broadcasted_iota(jnp.int32, shape, axis)


def fused(
    sizes,
    ids_ref, logits_ref, x_ref, g_ref, wg_hbm, wu_hbm, wd_hbm,
    tok_ref, gate_ref, up_ref, down_ref,
    ids_send, logits_pad, ids_all, ids_flat,
    wg, wu, wd,
    xcat, gcat, onehot, send_x, send_g, got_x, got_g,
    xs, xs_t, dy, act_t, coef1, coef3, dh1, dh3, gates,
    dx_cat, send_r, got_r,
    part_g, part_u, part_d0, part_d1,
    ring_g, ring_u, ring_d0, ring_d1,
    w_sem, ids_ssem, ids_rsem, fwd_ssem, fwd_rsem, own_sem, ret_ssem, ret_rsem,
    ring_ssem, ring_rsem,
):
    E, G, T, D, F, C = sizes
    Q = D // 4
    S = G // 2
    R4 = 4 * E
    BP = min(16, E)
    BR = BP * 16
    BO = BP * 4
    NB = E // BP
    factor = 1.0 / math.sqrt(G * 2 * C)
    me = lax.axis_index("expert")
    z = lax.axis_index("dp")
    z_right = lax.rem(z + 1, G)
    z_left = lax.rem(z + G - 1, G)

    weights = [
        pltpu.make_async_copy(src.at[0], dst, w_sem.at[k])
        for k, (src, dst) in enumerate(((wg_hbm, wg), (wu_hbm, wu), (wd_hbm, wd)))
    ]
    for copy in weights:
        copy.start()

    barrier = pltpu.get_barrier_semaphore()

    def greet(k, carry):
        pl.semaphore_signal(
            barrier, inc=1, device_id=(z, lax.rem(me + k, E)), device_id_type=MESH
        )
        return carry

    lax.fori_loop(1, E, greet, 0)
    for other in (z_right, z_left):
        pl.semaphore_signal(barrier, inc=1, device_id=(other, me), device_id_type=MESH)

    ids_send[...] = jnp.full(ids_send.shape, -1, jnp.int32)
    logits_pad[...] = jnp.zeros(logits_pad.shape, jnp.int32)
    for m in range(2):
        ids_send[m : m + 1, 0:C] = ids_ref[m, 0]
        logits_pad[m : m + 1, 0:C] = logits_ref[m, 0]
    ids_all[pl.ds(me, 1)] = ids_send[...][None]

    pl.semaphore_wait(barrier, E - 1 + 2)

    def send_ids(k, carry):
        pltpu.make_async_remote_copy(
            src_ref=ids_send,
            dst_ref=ids_all.at[me],
            send_sem=ids_ssem,
            recv_sem=ids_rsem,
            device_id=(z, lax.rem(me + k, E)),
            device_id_type=MESH,
        ).start()
        return carry

    lax.fori_loop(1, E, send_ids, 0)

    for m in range(2):
        for q in range(4):
            rows = pl.ds((q * 2 + m) * T, T)
            xcat[rows, :] = x_ref[m, :, q * Q : (q + 1) * Q]
            gcat[rows, :] = g_ref[m, :, q * Q : (q + 1) * Q]

    row = iota((R4, 128), 0)
    micro_row = (row // 2) % 2
    mine = jnp.where(micro_row == 0, ids_send[0:1, :], ids_send[1:2, :]).astype(F32)
    marks = jnp.where(micro_row == 0, logits_pad[0:1, :], logits_pad[1:2, :]).astype(F32)
    low = ((row // 4) * T).astype(F32)
    inside = (mine >= low) & (mine < low + float(T))
    first = jnp.min(jnp.where(inside, mine, 1e6), axis=1, keepdims=True)
    last = jnp.max(jnp.where(inside, mine, -1.0), axis=1, keepdims=True)
    pick = jnp.where(row % 2 == 0, first, last)
    logit = jnp.sum(jnp.where(inside & (mine == pick), marks, 0.0), axis=1, keepdims=True)
    gates[...] = jax.nn.sigmoid(logit * (1.0 / 4096.0))

    pltpu.make_async_copy(ids_all.at[pl.ds(0, E - 1)], ids_all.at[pl.ds(0, E - 1)], ids_rsem).wait()

    for e in range(E):
        for m in range(2):
            ids_flat[m, e : e + 1, :] = ids_all[e, m : m + 1, :]
    lane = iota((E, 128), 1)
    table = jnp.full((E, 128), -1.0, F32)
    base = (me * T).astype(F32)
    for m in range(2):
        local = ids_flat[m].astype(F32) - base
        inside = (local >= 0.0) & (local < float(T))
        first = jnp.min(jnp.where(inside, local, 1e6), axis=1, keepdims=True)
        last = jnp.max(jnp.where(inside, local, -1.0), axis=1, keepdims=True)
        first_ok = jnp.where(first < 1e5, first, -1.0)
        last_ok = jnp.where(last > first, last, -1.0)
        table = jnp.where(lane == 2 * m, first_ok, table)
        table = jnp.where(lane == 2 * m + 1, last_ok, table)
    table = table.astype(BF16)

    OB = min(128, E * 16)
    for blk in range(E * 16 // OB):
        rows = pl.ds(blk * OB, OB)
        spread = (
            (iota((OB, E), 0) + blk * OB) // 16 == iota((OB, E), 1)
        ).astype(F32).astype(BF16)
        values = jnp.dot(spread, table, preferred_element_type=F32)
        row = iota((OB, 128), 0)
        chosen = jnp.sum(
            jnp.where(iota((OB, 128), 1) == row % 4, values, 0.0), axis=1, keepdims=True
        )
        line = iota((OB, 1), 0)
        place = ((line // 4) % 4) * (2 * T) + ((line // 2) % 2) * T
        target = jnp.where(chosen < 0.0, -1.0, chosen + place.astype(F32))
        hot = (iota((OB, 8 * T), 1).astype(F32) == target).astype(F32).astype(BF16)
        onehot[rows, :] = hot
        send_x[rows, :] = jnp.dot(hot, xcat[...], preferred_element_type=F32).astype(BF16)

    def exchange(src, dst, ssem, rsem, osem):
        here = pl.ds(pl.multiple_of(me * 16, 16), 16)
        own = pltpu.make_async_copy(src.at[here], dst.at[here], osem)
        own.start()

        def one(k, carry):
            peer = lax.rem(me + k, E)
            pltpu.make_async_remote_copy(
                src_ref=src.at[pl.ds(pl.multiple_of(peer * 16, 16), 16)],
                dst_ref=dst.at[here],
                send_sem=ssem,
                recv_sem=rsem,
                device_id=(z, peer),
                device_id_type=MESH,
            ).start()
            return carry

        lax.fori_loop(1, E, one, 0)
        return own

    def arrived(dst, rsem, own):
        own.wait()
        whole = dst.at[pl.ds(0, (E - 1) * 16)]
        pltpu.make_async_copy(whole, whole, rsem).wait()

    own_x = exchange(send_x, got_x, fwd_ssem.at[0], fwd_rsem.at[0], own_sem.at[0])
    for blk in range(E * 16 // OB):
        rows = pl.ds(blk * OB, OB)
        send_g[rows, :] = jnp.dot(
            onehot[rows, :], gcat[...], preferred_element_type=F32
        ).astype(BF16)
    own_g = exchange(send_g, got_g, fwd_ssem.at[1], fwd_rsem.at[1], own_sem.at[1])

    r = iota((BR, BR), 0)
    c = iota((BR, BR), 1)
    perm = (
        c == ((r // 4) % BP) * 16 + (r // BO) * 4 + r % 4
    ).astype(F32).astype(BF16)
    perm_t = (
        r == ((c // 4) % BP) * 16 + (c // BO) * 4 + c % 4
    ).astype(F32).astype(BF16)

    for copy in weights:
        copy.wait()
    arrived(got_x, fwd_rsem.at[0], own_x)
    for blk in range(NB):
        moved = jnp.dot(perm, got_x[blk * BR : (blk + 1) * BR, :], preferred_element_type=F32)
        for q in range(4):
            xs[blk * BO : (blk + 1) * BO, q * Q : (q + 1) * Q] = moved[
                q * BO : (q + 1) * BO
            ].astype(BF16)
    FT = min(256, F)
    for ft in range(F // FT):
        cols = slice(ft * FT, (ft + 1) * FT)
        h1 = jnp.dot(xs[...], wg[:, cols], preferred_element_type=F32)
        h3 = jnp.dot(xs[...], wu[:, cols], preferred_element_type=F32)
        sig = jax.nn.sigmoid(h1)
        gated = h1 * sig
        act_t[cols, :] = (gated * h3).astype(BF16).T
        coef3[:, cols] = gated
        coef1[:, cols] = h3 * sig * (1.0 + h1 * (1.0 - sig))
    for q in range(4):
        xs_t[q * Q : (q + 1) * Q, :] = xs[:, q * Q : (q + 1) * Q].T

    arrived(got_g, fwd_rsem.at[1], own_g)
    for blk in range(NB):
        moved = jnp.dot(perm, got_g[blk * BR : (blk + 1) * BR, :], preferred_element_type=F32)
        scale = gates[blk * BO : (blk + 1) * BO, :]
        for q in range(4):
            dy[blk * BO : (blk + 1) * BO, q * Q : (q + 1) * Q] = (
                moved[q * BO : (q + 1) * BO] * scale
            ).astype(BF16)

    parts = (part_g, part_u, part_d0, part_d1)
    rings = (ring_g, ring_u, ring_d0, ring_d1)
    heights = (D // G, D // G, F // G, F // G)
    starts = ((0, 1, 0, 1), (1, 0, 1, 0))

    def piece(p, chunk):
        return pl.ds(pl.multiple_of(chunk * heights[p], heights[p]), heights[p])

    def forward(way, p, step, src):
        pltpu.make_async_remote_copy(
            src_ref=src,
            dst_ref=rings[p].at[way, step],
            send_sem=ring_ssem.at[way, p, step],
            recv_sem=ring_rsem.at[way, p, step],
            device_id=(z_right if way == 0 else z_left, me),
            device_id_type=MESH,
        ).start()

    def ring_copy(way, p, step):
        return pltpu.make_async_remote_copy(
            src_ref=rings[p].at[way, step],
            dst_ref=rings[p].at[way, step],
            send_sem=ring_ssem.at[way, p, step],
            recv_sem=ring_rsem.at[way, p, step],
            device_id=(z_right if way == 0 else z_left, me),
            device_id_type=MESH,
        )

    far = lax.rem(z + S, G)

    def begin(p):
        forward(starts[0][p], p, 0, parts[p].at[piece(p, far)])

    for ft in range(F // FT):
        rows = slice(ft * FT, (ft + 1) * FT)
        for half, part in ((0, part_d0), (1, part_d1)):
            part[rows, :] = (
                jnp.dot(
                    act_t[rows, :],
                    dy[:, half * (D // 2) : (half + 1) * (D // 2)],
                    preferred_element_type=F32,
                )
                * factor
            ).astype(BF16)
    begin(2)
    begin(3)
    for ft in range(F // FT):
        cols = slice(ft * FT, (ft + 1) * FT)
        dact = lax.dot_general(dy[...], wd[cols, :], contract_cols, preferred_element_type=F32)
        dh1[:, cols] = (dact * coef1[:, cols]).astype(BF16)
        dh3[:, cols] = (dact * coef3[:, cols]).astype(BF16)
    for p, part, dh in ((0, part_g, dh1), (1, part_u, dh3)):
        for q in range(4):
            rows = slice(q * Q, (q + 1) * Q)
            part[rows, :] = (
                jnp.dot(xs_t[rows, :], dh[...], preferred_element_type=F32) * factor
            ).astype(BF16)
        begin(p)

    def chunk_at(way, step):
        if way == 0:
            return lax.rem(z + S - step + G, G)
        return lax.rem(z + S + step, G)

    def pass_on(way, p, step):
        ring_copy(way, p, step - 1).wait_recv()
        held = rings[p].at[way, step - 1]
        held[...] = (
            held[...].astype(F32) + parts[p][piece(p, chunk_at(way, step)), :].astype(F32)
        ).astype(BF16)
        forward(way, p, step, held)

    order = ((0, 2), (1, 3), (0, 0), (1, 1), (0, 3), (1, 2), (0, 1), (1, 0))
    for way, p in order:
        if starts[way][p] == 1:
            forward(way, p, 1, parts[p].at[piece(p, chunk_at(way, 1))])
    for way, p in order:
        if starts[way][p] == 0:
            pass_on(way, p, 1)

    for q in range(4):
        rows = slice(q * Q, (q + 1) * Q)
        dx = (
            lax.dot_general(dh1[...], wg[rows, :], contract_cols, preferred_element_type=F32)
            + lax.dot_general(dh3[...], wu[rows, :], contract_cols, preferred_element_type=F32)
        ).astype(BF16)
        for blk in range(NB):
            dx_cat[blk * BR + q * BO : blk * BR + (q + 1) * BO, :] = dx[blk * BO : (blk + 1) * BO]
    for blk in range(NB):
        rows = slice(blk * BR, (blk + 1) * BR)
        send_r[rows, :] = jnp.dot(
            perm_t, dx_cat[rows, :], preferred_element_type=F32
        ).astype(BF16)
    own_r = exchange(send_r, got_r, ret_ssem, ret_rsem, own_sem.at[2])

    def ring_step(step, carry):
        for way, p in order:
            pass_on(way, p, step)
        return carry

    lax.fori_loop(2, S, ring_step, 0)

    arrived(got_r, ret_rsem, own_r)
    summed = lax.dot_general(onehot[...], got_r[...], contract_rows, preferred_element_type=F32)
    for m in range(2):
        for q in range(4):
            tok_ref[m, :, q * Q : (q + 1) * Q] = summed[
                (q * 2 + m) * T : (q * 2 + m + 1) * T
            ].astype(BF16)

    def finish(p):
        ring_copy(0, p, S - 1).wait_recv()
        ring_copy(1, p, S - 1).wait_recv()
        return (
            rings[p][0, S - 1].astype(F32)
            + rings[p][1, S - 1].astype(F32)
            + parts[p][piece(p, z), :].astype(F32)
        ).astype(BF16)

    down_ref[0, :, 0 : D // 2] = finish(2)
    down_ref[0, :, D // 2 : D] = finish(3)
    gate_ref[0] = finish(0)
    up_ref[0] = finish(1)

    pltpu.make_async_copy(ids_all.at[pl.ds(0, E - 1)], ids_all.at[pl.ds(0, E - 1)], ids_ssem).wait()
    for src, sem in ((send_x, fwd_ssem.at[0]), (send_g, fwd_ssem.at[1]), (send_r, ret_ssem)):
        whole = src.at[pl.ds(0, (E - 1) * 16)]
        pltpu.make_async_copy(whole, whole, sem).wait()
    for way in range(2):
        for p in range(4):
            for step in range(starts[way][p], S):
                ring_copy(way, p, step).wait_send()


def body(activations, out_grads, chosen_ids, gate_logits, w_gate, w_up, w_down):
    E = lax.axis_size("expert")
    G = lax.axis_size("dp")
    T, D = activations.shape[1:]
    F = w_gate.shape[-1]
    C = chosen_ids.shape[-1]
    Q, S, R4, R16 = D // 4, G // 2, 4 * E, 16 * E
    vmem = pl.BlockSpec(memory_space=pltpu.VMEM)
    anywhere = pl.BlockSpec(memory_space=pl.ANY)
    V = pltpu.VMEM
    dma = pltpu.SemaphoreType.DMA
    scratch = [
        V((2, 128), jnp.int32), V((2, 128), jnp.int32),
        V((E, 2, 128), jnp.int32), V((2, E, 128), jnp.int32),
        V((D, F), BF16), V((D, F), BF16), V((F, D), BF16),
        V((8 * T, Q), BF16), V((8 * T, Q), BF16), V((R16, 8 * T), BF16),
        V((R16, Q), BF16), V((R16, Q), BF16), V((R16, Q), BF16), V((R16, Q), BF16),
        V((R4, D), BF16), V((D, R4), BF16), V((R4, D), BF16), V((F, R4), BF16),
        V((R4, F), F32), V((R4, F), F32), V((R4, F), BF16), V((R4, F), BF16), V((R4, 1), F32),
        V((R16, Q), BF16), V((R16, Q), BF16), V((R16, Q), BF16),
        V((D, F), BF16), V((D, F), BF16), V((F, D // 2), BF16), V((F, D // 2), BF16),
        V((2, S, D // G, F), BF16), V((2, S, D // G, F), BF16),
        V((2, S, F // G, D // 2), BF16), V((2, S, F // G, D // 2), BF16),
        dma((3,)), dma, dma, dma((2,)), dma((2,)), dma((3,)), dma, dma,
        dma((2, 4, S)), dma((2, 4, S)),
    ]
    shape = jax.ShapeDtypeStruct
    return pl.pallas_call(
        functools.partial(fused, (E, G, T, D, F, C)),
        out_shape=(
            shape((2, T, D), BF16),
            shape((1, D // G, F), BF16),
            shape((1, D // G, F), BF16),
            shape((1, F // G, D), BF16),
        ),
        in_specs=[vmem, vmem, vmem, vmem, anywhere, anywhere, anywhere],
        out_specs=(vmem, vmem, vmem, vmem),
        scratch_shapes=scratch,
        compiler_params=pltpu.CompilerParams(
            collective_id=0, has_side_effects=True, vmem_limit_bytes=48 * 1024 * 1024
        ),
    )(chosen_ids, gate_logits, activations, out_grads, w_gate, w_up, w_down)


def solution(mesh):
    placed = (
        P(None, ("dp", "expert"), None),
        P(None, ("dp", "expert"), None),
        P(None, "dp", "expert", None),
        P(None, "dp", "expert", None),
        P("expert", None, None),
        P("expert", None, None),
        P("expert", None, None),
    )
    return jax.shard_map(
        body,
        mesh=mesh,
        in_specs=placed,
        out_specs=(
            P(None, ("dp", "expert"), None),
            P("expert", "dp", None),
            P("expert", "dp", None),
            P("expert", "dp", None),
        ),
        check_vma=False,
    )
```

time: 368 us -> 120 us (0.33)
  the two profiles are of different devices: /device:TPU:2 before, /device:TPU:1 now
where the time goes in v1:
time: 120 us
  Pallas kernels  109 us (91%)
  local copies, waits for them, and re-layouts  10 us (8%)
    pallas_call x1, Pallas kernels, body(): pl.pallas_call(functools.partial(fused, (E, G, T, D, F, C)), out_shape=(s...  109 us
    unnamed x18, local copies, waits for them, and re-layouts  10 us

profile of v1, /device:TPU:1, one launch (start us, length us, event | category | flops | bytes accessed | tf_op | source)
XLA Modules:
  0.0 119.6 jit_solution(17970213502486432284)
XLA Ops:
  0.6 0.0 copy-start
  0.6 1.4 %copy-done = bf16[1,1024,768]{2,1,0:T(8,128)(2,1)S(1)} copy-done((bf16[1,1024,768]{2,1,0:T(8,128)(2,1)S(1)}, bf16[1,1024,768]{2,1,0:T(8,128)(2,1)}, u32[]{:S(2)}) %copy-start) | copy-done | bytes 1572888
  2.0 0.0 copy-start.1
  2.0 1.4 %copy-done.1 = bf16[1,1024,768]{2,1,0:T(8,128)(2,1)S(1)} copy-done((bf16[1,1024,768]{2,1,0:T(8,128)(2,1)S(1)}, bf16[1,1024,768]{2,1,0:T(8,128)(2,1)}, u32[]{:S(2)}) %copy-start.1) | copy-done | bytes 1572888
  3.5 0.0 copy-start.2
  3.5 1.4 %copy-done.2 = bf16[1,768,1024]{2,1,0:T(8,128)(2,1)S(1)} copy-done((bf16[1,768,1024]{2,1,0:T(8,128)(2,1)S(1)}, bf16[1,768,1024]{2,1,0:T(8,128)(2,1)}, u32[]{:S(2)}) %copy-start.2) | copy-done | bytes 1572888
  4.9 0.0 copy-start.3
  4.9 0.9 copy-done.3
  5.8 0.0 copy-start.4
  5.8 0.9 copy-done.4
  6.7 0.0 copy-start.5
  6.7 0.7 copy-done.5
  7.4 0.0 copy-start.6
  7.4 0.7 copy-done.6
  8.1 108.9 %shard_map.102 = (bf16[2,48,1024]{2,1,0:T(8,128)(2,1)S(1)}, bf16[1,64,768]{2,1,0:T(8,128)(2,1)S(1)}, bf16[1,64,768]{2,1,0:T(8,128)(2,1)S(1)}, bf16[1,48,1024]{2,1,0:T(8,128)(2,1)S(1)}) custom-call(s32[2,1,1,96]{3,2,1,0:T(1,128)S(1)} %copy-done.5, s32[2,1,1,96]{3,2,1,0:T(1,128)S(1)} %copy-done.6, bf16[2,48,1024]{2,1,0:T(8,128)(2,1)S(1)} %copy-done.3, ...), custom_call_target="tpu_custom_call" | custom-call | tf_op jit(solution)/shard_map/pallas_call | solution.py:380
  116.9 0.7 copy.15
  117.6 0.6 copy.16
  118.3 0.6 copy.17
  118.9 0.6 copy.18
Async XLA Ops:
  0.6 1.4 %copy-start = (bf16[1,1024,768]{2,1,0:T(8,128)(2,1)S(1)}, bf16[1,1024,768]{2,1,0:T(8,128)(2,1)}, u32[]{:S(2)}) copy-start(bf16[1,1024,768]{2,1,0:T(8,128)(2,1)} %wg_hbm.1) | copy-start | bytes 4718596
  2.0 1.4 %copy-start.1 = (bf16[1,1024,768]{2,1,0:T(8,128)(2,1)S(1)}, bf16[1,1024,768]{2,1,0:T(8,128)(2,1)}, u32[]{:S(2)}) copy-start(bf16[1,1024,768]{2,1,0:T(8,128)(2,1)} %wu_hbm.1) | copy-start | bytes 4718596
  3.5 1.4 %copy-start.2 = (bf16[1,768,1024]{2,1,0:T(8,128)(2,1)S(1)}, bf16[1,768,1024]{2,1,0:T(8,128)(2,1)}, u32[]{:S(2)}) copy-start(bf16[1,768,1024]{2,1,0:T(8,128)(2,1)} %wd_hbm.1) | copy-start | bytes 4718596
  4.9 0.9 copy-start.3
  5.8 0.9 copy-start.4
  6.7 0.7 copy-start.5
  7.4 0.7 copy-start.6

commit v2 on v1

--- a/solution.py
+++ b/solution.py
@@ -21,16 +21,16 @@
 
 def fused(
     sizes,
-    ids_ref, logits_ref, x_ref, g_ref, wg_hbm, wu_hbm, wd_hbm,
+    ids_hbm, logits_hbm, x_hbm, g_hbm, wg_hbm, wu_hbm, wd_hbm,
     tok_ref, gate_ref, up_ref, down_ref,
-    ids_send, logits_pad, ids_all, ids_flat,
+    ids_ref, logits_ref, ids_send, logits_pad, ids_all, ids_flat,
     wg, wu, wd,
-    xcat, gcat, onehot, send_x, send_g, got_x, got_g,
+    xcat, gcat, onehot, send_x, send_g, got_x, got_g, dacc,
     xs, xs_t, dy, act_t, coef1, coef3, dh1, dh3, gates,
     dx_cat, send_r, got_r,
     part_g, part_u, part_d0, part_d1,
     ring_g, ring_u, ring_d0, ring_d1,
-    w_sem, ids_ssem, ids_rsem, fwd_ssem, fwd_rsem, own_sem, ret_ssem, ret_rsem,
+    w_sem, in_sem, ids_ssem, ids_rsem, fwd_ssem, fwd_rsem, own_sem, ret_ssem, ret_rsem,
     ring_ssem, ring_rsem,
 ):
     E, G, T, D, F, C = sizes
@@ -47,24 +47,49 @@
     z_right = lax.rem(z + 1, G)
     z_left = lax.rem(z + G - 1, G)
 
+    RW = min(8, E // 2)
+    CW = E // RW
+    row_at = me // RW
+    col_at = lax.rem(me, RW)
+
+    small = [
+        pltpu.make_async_copy(src, dst, in_sem.at[k])
+        for k, (src, dst) in enumerate(((ids_hbm, ids_ref), (logits_hbm, logits_ref)))
+    ]
+    for copy in small:
+        copy.start()
+
+    def row_mate(k):
+        return row_at * RW + lax.rem(col_at + k, RW)
+
+    def col_mate(k):
+        return lax.rem(row_at + k, CW) * RW + col_at
+
+    barrier = pltpu.get_barrier_semaphore()
+    mates = [(z, row_mate(k)) for k in range(1, RW)] + [(z, col_mate(k)) for k in range(1, CW)]
+    for other in mates + [(z_right, me), (z_left, me)]:
+        pl.semaphore_signal(barrier, inc=1, device_id=other, device_id_type=MESH)
+
+    for m in range(2):
+        for q in range(4):
+            rows = pl.ds((q * 2 + m) * T, T)
+            pltpu.make_async_copy(
+                x_hbm.at[m, :, pl.ds(q * Q, Q)], xcat.at[rows, :], in_sem.at[2]
+            ).start()
+            for half in range(2):
+                pltpu.make_async_copy(
+                    g_hbm.at[m, :, pl.ds(half * (D // 2) + q * (Q // 2), Q // 2)],
+                    gcat.at[half, rows, :],
+                    in_sem.at[3],
+                ).start()
     weights = [
         pltpu.make_async_copy(src.at[0], dst, w_sem.at[k])
         for k, (src, dst) in enumerate(((wg_hbm, wg), (wu_hbm, wu), (wd_hbm, wd)))
     ]
     for copy in weights:
         copy.start()
-
-    barrier = pltpu.get_barrier_semaphore()
-
-    def greet(k, carry):
-        pl.semaphore_signal(
-            barrier, inc=1, device_id=(z, lax.rem(me + k, E)), device_id_type=MESH
-        )
-        return carry
-
-    lax.fori_loop(1, E, greet, 0)
-    for other in (z_right, z_left):
-        pl.semaphore_signal(barrier, inc=1, device_id=(other, me), device_id_type=MESH)
+    for copy in small:
+        copy.wait()
 
     ids_send[...] = jnp.full(ids_send.shape, -1, jnp.int32)
     logits_pad[...] = jnp.zeros(logits_pad.shape, jnp.int32)
@@ -73,26 +98,30 @@
         logits_pad[m : m + 1, 0:C] = logits_ref[m, 0]
     ids_all[pl.ds(me, 1)] = ids_send[...][None]
 
-    pl.semaphore_wait(barrier, E - 1 + 2)
-
-    def send_ids(k, carry):
+    pl.semaphore_wait(barrier, RW - 1 + CW - 1 + 2)
+
+    for k in range(1, RW):
         pltpu.make_async_remote_copy(
             src_ref=ids_send,
             dst_ref=ids_all.at[me],
-            send_sem=ids_ssem,
-            recv_sem=ids_rsem,
-            device_id=(z, lax.rem(me + k, E)),
+            send_sem=ids_ssem.at[0],
+            recv_sem=ids_rsem.at[0],
+            device_id=(z, row_mate(k)),
             device_id_type=MESH,
         ).start()
-        return carry
-
-    lax.fori_loop(1, E, send_ids, 0)
-
-    for m in range(2):
-        for q in range(4):
-            rows = pl.ds((q * 2 + m) * T, T)
-            xcat[rows, :] = x_ref[m, :, q * Q : (q + 1) * Q]
-            gcat[rows, :] = g_ref[m, :, q * Q : (q + 1) * Q]
+    near = ids_all.at[pl.ds(0, max(RW - 1, 1))]
+    if RW > 1:
+        pltpu.make_async_copy(near, near, ids_rsem.at[0]).wait()
+    ours = ids_all.at[pl.ds(row_at * RW, RW)]
+    for k in range(1, CW):
+        pltpu.make_async_remote_copy(
+            src_ref=ours,
+            dst_ref=ours,
+            send_sem=ids_ssem.at[1],
+            recv_sem=ids_rsem.at[1],
+            device_id=(z, col_mate(k)),
+            device_id_type=MESH,
+        ).start()
 
     row = iota((R4, 128), 0)
     micro_row = (row // 2) % 2
@@ -106,7 +135,8 @@
     logit = jnp.sum(jnp.where(inside & (mine == pick), marks, 0.0), axis=1, keepdims=True)
     gates[...] = jax.nn.sigmoid(logit * (1.0 / 4096.0))
 
-    pltpu.make_async_copy(ids_all.at[pl.ds(0, E - 1)], ids_all.at[pl.ds(0, E - 1)], ids_rsem).wait()
+    rest = ids_all.at[pl.ds(0, (CW - 1) * RW)]
+    pltpu.make_async_copy(rest, rest, ids_rsem.at[1]).wait()
 
     for e in range(E):
         for m in range(2):
@@ -126,6 +156,7 @@
     table = table.astype(BF16)
 
     OB = min(128, E * 16)
+    pltpu.make_async_copy(xcat, xcat, in_sem.at[2]).wait()
     for blk in range(E * 16 // OB):
         rows = pl.ds(blk * OB, OB)
         spread = (
@@ -143,11 +174,14 @@
         onehot[rows, :] = hot
         send_x[rows, :] = jnp.dot(hot, xcat[...], preferred_element_type=F32).astype(BF16)
 
-    def exchange(src, dst, ssem, rsem, osem):
-        here = pl.ds(pl.multiple_of(me * 16, 16), 16)
+    here = pl.ds(pl.multiple_of(me * 16, 16), 16)
+
+    def keep(src, dst, osem):
         own = pltpu.make_async_copy(src.at[here], dst.at[here], osem)
         own.start()
-
+        return own
+
+    def exchange(src, dst, ssem, rsem, begin_at=1, end_at=E):
         def one(k, carry):
             peer = lax.rem(me + k, E)
             pltpu.make_async_remote_copy(
@@ -160,21 +194,26 @@
             ).start()
             return carry
 
-        lax.fori_loop(1, E, one, 0)
-        return own
+        lax.fori_loop(begin_at, end_at, one, 0)
 
     def arrived(dst, rsem, own):
         own.wait()
         whole = dst.at[pl.ds(0, (E - 1) * 16)]
         pltpu.make_async_copy(whole, whole, rsem).wait()
 
-    own_x = exchange(send_x, got_x, fwd_ssem.at[0], fwd_rsem.at[0], own_sem.at[0])
-    for blk in range(E * 16 // OB):
-        rows = pl.ds(blk * OB, OB)
-        send_g[rows, :] = jnp.dot(
-            onehot[rows, :], gcat[...], preferred_element_type=F32
-        ).astype(BF16)
-    own_g = exchange(send_g, got_g, fwd_ssem.at[1], fwd_rsem.at[1], own_sem.at[1])
+    exchange(send_x, got_x, fwd_ssem.at[0], fwd_rsem.at[0])
+    own_x = keep(send_x, got_x, own_sem.at[0])
+    own_g = []
+    pltpu.make_async_copy(gcat, gcat, in_sem.at[3]).wait()
+    for half in range(2):
+        for blk in range(E * 16 // OB):
+            rows = pl.ds(blk * OB, OB)
+            send_g[half, rows, :] = jnp.dot(
+                onehot[rows, :], gcat[half], preferred_element_type=F32
+            ).astype(BF16)
+        src, dst = send_g.at[half], got_g.at[half]
+        exchange(src, dst, fwd_ssem.at[1 + half], fwd_rsem.at[1 + half])
+        own_g.append(keep(src, dst, own_sem.at[1 + half]))
 
     r = iota((BR, BR), 0)
     c = iota((BR, BR), 1)
@@ -207,14 +246,18 @@
     for q in range(4):
         xs_t[q * Q : (q + 1) * Q, :] = xs[:, q * Q : (q + 1) * Q].T
 
-    arrived(got_g, fwd_rsem.at[1], own_g)
-    for blk in range(NB):
-        moved = jnp.dot(perm, got_g[blk * BR : (blk + 1) * BR, :], preferred_element_type=F32)
-        scale = gates[blk * BO : (blk + 1) * BO, :]
-        for q in range(4):
-            dy[blk * BO : (blk + 1) * BO, q * Q : (q + 1) * Q] = (
-                moved[q * BO : (q + 1) * BO] * scale
-            ).astype(BF16)
+    def take_grads(half):
+        arrived(got_g.at[half], fwd_rsem.at[1 + half], own_g[half])
+        for blk in range(NB):
+            moved = jnp.dot(
+                perm, got_g[half, blk * BR : (blk + 1) * BR, :], preferred_element_type=F32
+            )
+            scale = gates[blk * BO : (blk + 1) * BO, :]
+            for q in range(4):
+                left = half * (D // 2) + q * (Q // 2)
+                dy[blk * BO : (blk + 1) * BO, left : left + Q // 2] = (
+                    moved[q * BO : (q + 1) * BO] * scale
+                ).astype(BF16)
 
     parts = (part_g, part_u, part_d0, part_d1)
     rings = (ring_g, ring_u, ring_d0, ring_d1)
@@ -244,27 +287,55 @@
             device_id_type=MESH,
         )
 
-    far = lax.rem(z + S, G)
-
-    def begin(p):
-        forward(starts[0][p], p, 0, parts[p].at[piece(p, far)])
-
-    for ft in range(F // FT):
-        rows = slice(ft * FT, (ft + 1) * FT)
-        for half, part in ((0, part_d0), (1, part_d1)):
-            part[rows, :] = (
-                jnp.dot(
-                    act_t[rows, :],
-                    dy[:, half * (D // 2) : (half + 1) * (D // 2)],
-                    preferred_element_type=F32,
-                )
-                * factor
+    def chunk_at(way, step):
+        if way == 0:
+            return lax.rem(z + S - step + G, G)
+        return lax.rem(z + S + step, G)
+
+    def pass_on(way, p, step):
+        ring_copy(way, p, step - 1).wait_recv()
+        held = rings[p].at[way, step - 1]
+        held[...] = (
+            held[...].astype(F32) + parts[p][piece(p, chunk_at(way, step)), :].astype(F32)
+        ).astype(BF16)
+        forward(way, p, step, held)
+
+    halves = (slice(0, D // 2), slice(D // 2, D))
+
+    def down_part(half):
+        for ft in range(F // FT):
+            rows = slice(ft * FT, (ft + 1) * FT)
+            parts[2 + half][rows, :] = (
+                jnp.dot(act_t[rows, :], dy[:, halves[half]], preferred_element_type=F32) * factor
             ).astype(BF16)
-    begin(2)
-    begin(3)
+
+    def enter(way, p):
+        step = starts[way][p]
+        forward(way, p, step, parts[p].at[piece(p, chunk_at(way, step))])
+
+    take_grads(0)
+    down_part(0)
+    enter(0, 2)
+    enter(1, 2)
     for ft in range(F // FT):
         cols = slice(ft * FT, (ft + 1) * FT)
-        dact = lax.dot_general(dy[...], wd[cols, :], contract_cols, preferred_element_type=F32)
+        dacc[:, cols] = lax.dot_general(
+            dy[:, halves[0]], wd[cols, halves[0]], contract_cols, preferred_element_type=F32
+        )
+    pass_on(0, 2, 1)
+    if S > 2:
+        pass_on(0, 2, 2)
+        pass_on(1, 2, 2)
+
+    take_grads(1)
+    down_part(1)
+    enter(1, 3)
+    enter(0, 3)
+    for ft in range(F // FT):
+        cols = slice(ft * FT, (ft + 1) * FT)
+        dact = dacc[:, cols] + lax.dot_general(
+            dy[:, halves[1]], wd[cols, halves[1]], contract_cols, preferred_element_type=F32
+        )
         dh1[:, cols] = (dact * coef1[:, cols]).astype(BF16)
         dh3[:, cols] = (dact * coef3[:, cols]).astype(BF16)
     for p, part, dh in ((0, part_g, dh1), (1, part_u, dh3)):
@@ -273,28 +344,14 @@
             part[rows, :] = (
                 jnp.dot(xs_t[rows, :], dh[...], preferred_element_type=F32) * factor
             ).astype(BF16)
-        begin(p)
-
-    def chunk_at(way, step):
-        if way == 0:
-            return lax.rem(z + S - step + G, G)
-        return lax.rem(z + S + step, G)
-
-    def pass_on(way, p, step):
-        ring_copy(way, p, step - 1).wait_recv()
-        held = rings[p].at[way, step - 1]
-        held[...] = (
-            held[...].astype(F32) + parts[p][piece(p, chunk_at(way, step)), :].astype(F32)
-        ).astype(BF16)
-        forward(way, p, step, held)
-
-    order = ((0, 2), (1, 3), (0, 0), (1, 1), (0, 3), (1, 2), (0, 1), (1, 0))
-    for way, p in order:
-        if starts[way][p] == 1:
-            forward(way, p, 1, parts[p].at[piece(p, chunk_at(way, 1))])
-    for way, p in order:
-        if starts[way][p] == 0:
-            pass_on(way, p, 1)
+        enter(p, p)
+        enter(1 - p, p)
+    if S > 3:
+        pass_on(0, 2, 3)
+        pass_on(1, 2, 3)
+    order = ((1, 3), (0, 0), (1, 1), (0, 3), (1, 0), (0, 1))
+    for way, p in order[:3]:
+        pass_on(way, p, 1)
 
     for q in range(4):
         rows = slice(q * Q, (q + 1) * Q)
@@ -309,14 +366,31 @@
         send_r[rows, :] = jnp.dot(
             perm_t, dx_cat[rows, :], preferred_element_type=F32
         ).astype(BF16)
-    own_r = exchange(send_r, got_r, ret_ssem, ret_rsem, own_sem.at[2])
+    own_r = keep(send_r, got_r, own_sem.at[3])
+    lead = max(S - 4, 0)
+    per = -(-(E - 1) // max(lead, 1))
 
     def ring_step(step, carry):
+        for way, p in order[:3]:
+            pass_on(way, p, step)
+        begin_at = 1 + (step - 2) * per
+        exchange(send_r, got_r, ret_ssem, ret_rsem, begin_at, jnp.minimum(begin_at + per, E))
+        for way in range(2):
+            pass_on(way, 2, step + 2)
+        for way, p in order[3:]:
+            pass_on(way, p, step)
+        return carry
+
+    def last_steps(step, carry):
         for way, p in order:
             pass_on(way, p, step)
         return carry
 
-    lax.fori_loop(2, S, ring_step, 0)
+    if lead:
+        lax.fori_loop(2, 2 + lead, ring_step, 0)
+    else:
+        exchange(send_r, got_r, ret_ssem, ret_rsem)
+    lax.fori_loop(2 + lead, S, last_steps, 0)
 
     arrived(got_r, ret_rsem, own_r)
     summed = lax.dot_general(onehot[...], got_r[...], contract_rows, preferred_element_type=F32)
@@ -340,8 +414,11 @@
     gate_ref[0] = finish(0)
     up_ref[0] = finish(1)
 
-    pltpu.make_async_copy(ids_all.at[pl.ds(0, E - 1)], ids_all.at[pl.ds(0, E - 1)], ids_ssem).wait()
-    for src, sem in ((send_x, fwd_ssem.at[0]), (send_g, fwd_ssem.at[1]), (send_r, ret_ssem)):
+    if RW > 1:
+        pltpu.make_async_copy(near, near, ids_ssem.at[0]).wait()
+    pltpu.make_async_copy(rest, rest, ids_ssem.at[1]).wait()
+    sent = [(send_g.at[half], fwd_ssem.at[1 + half]) for half in range(2)]
+    for src, sem in [(send_x, fwd_ssem.at[0]), (send_r, ret_ssem)] + sent:
         whole = src.at[pl.ds(0, (E - 1) * 16)]
         pltpu.make_async_copy(whole, whole, sem).wait()
     for way in range(2):
@@ -358,22 +435,24 @@
     C = chosen_ids.shape[-1]
     Q, S, R4, R16 = D // 4, G // 2, 4 * E, 16 * E
     vmem = pl.BlockSpec(memory_space=pltpu.VMEM)
-    anywhere = pl.BlockSpec(memory_space=pl.ANY)
+    hbm = pl.BlockSpec(memory_space=pltpu.HBM)
     V = pltpu.VMEM
     dma = pltpu.SemaphoreType.DMA
     scratch = [
+        V((2, 1, 1, C), jnp.int32), V((2, 1, 1, C), jnp.int32),
         V((2, 128), jnp.int32), V((2, 128), jnp.int32),
         V((E, 2, 128), jnp.int32), V((2, E, 128), jnp.int32),
         V((D, F), BF16), V((D, F), BF16), V((F, D), BF16),
-        V((8 * T, Q), BF16), V((8 * T, Q), BF16), V((R16, 8 * T), BF16),
-        V((R16, Q), BF16), V((R16, Q), BF16), V((R16, Q), BF16), V((R16, Q), BF16),
+        V((8 * T, Q), BF16), V((2, 8 * T, Q // 2), BF16), V((R16, 8 * T), BF16),
+        V((R16, Q), BF16), V((2, R16, Q // 2), BF16),
+        V((R16, Q), BF16), V((2, R16, Q // 2), BF16), V((R4, F), F32),
         V((R4, D), BF16), V((D, R4), BF16), V((R4, D), BF16), V((F, R4), BF16),
         V((R4, F), F32), V((R4, F), F32), V((R4, F), BF16), V((R4, F), BF16), V((R4, 1), F32),
         V((R16, Q), BF16), V((R16, Q), BF16), V((R16, Q), BF16),
         V((D, F), BF16), V((D, F), BF16), V((F, D // 2), BF16), V((F, D // 2), BF16),
         V((2, S, D // G, F), BF16), V((2, S, D // G, F), BF16),
         V((2, S, F // G, D // 2), BF16), V((2, S, F // G, D // 2), BF16),
-        dma((3,)), dma, dma, dma((2,)), dma((2,)), dma((3,)), dma, dma,
+        dma((3,)), dma((4,)), dma((2,)), dma((2,)), dma((3,)), dma((3,)), dma((4,)), dma, dma,
         dma((2, 4, S)), dma((2, 4, S)),
     ]
     shape = jax.ShapeDtypeStruct
@@ -385,11 +464,11 @@
             shape((1, D // G, F), BF16),
             shape((1, F // G, D), BF16),
         ),
-        in_specs=[vmem, vmem, vmem, vmem, anywhere, anywhere, anywhere],
+        in_specs=[hbm] * 7,
         out_specs=(vmem, vmem, vmem, vmem),
         scratch_shapes=scratch,
         compiler_params=pltpu.CompilerParams(
-            collective_id=0, has_side_effects=True, vmem_limit_bytes=48 * 1024 * 1024
+            collective_id=0, has_side_effects=True, vmem_limit_bytes=64 * 1024 * 1024
         ),
     )(chosen_ids, gate_logits, activations, out_grads, w_gate, w_up, w_down)
 

time: 120 us -> 121 us (level)
  the two profiles are of different devices: /device:TPU:1 before, /device:TPU:6 now
where the time goes in v2:
time: 121 us; the launch traced here: 120 us
  Pallas kernels  113 us (93%)
  local copies, waits for them, and re-layouts  6.23 us (5%)
    pallas_call x1, Pallas kernels, body(): pl.pallas_call(functools.partial(fused, (E, G, T, D, F, C)), out_shape=(s...  113 us
    unnamed x4, local copies, waits for them, and re-layouts  6.23 us

profile of v2, /device:TPU:6, one launch (start us, length us, event | category | flops | bytes accessed | tf_op | source)
XLA Modules:
  0.0 120.3 jit_solution(1762377263727378563)
XLA Ops:
  0.6 113.4 %shard_map.102 = (bf16[2,48,1024]{2,1,0:T(8,128)(2,1)}, bf16[1,64,768]{2,1,0:T(8,128)(2,1)}, bf16[1,64,768]{2,1,0:T(8,128)(2,1)}, bf16[1,48,1024]{2,1,0:T(8,128)(2,1)}) custom-call(s32[2,1,1,96]{3,2,1,0:T(1,128)} %ids_hbm.1, s32[2,1,1,96]{3,2,1,0:T(1,128)} %logits_hbm.1, bf16[2,48,1024]{2,1,0:T(8,128)(2,1)} %x_hbm.1, bf16[2,48,1024]{2,1,0:T(8,128)(2,1)} %g_hbm.1, ...), custom_call_target="tpu_custom_call" | custom-call | tf_op jit(solution)/shard_map/pallas_call | solution.py:459
  114.1 1.6 %copy.15 = bf16[2,48,1024]{2,1,0:T(8,128)(2,1)} copy(bf16[2,48,1024]{2,1,0:T(8,128)(2,1)} %get-tuple-element.8) | data formatting | bytes 393216
  115.7 1.5 %copy.16 = bf16[1,64,768]{2,1,0:T(8,128)(2,1)} copy(bf16[1,64,768]{2,1,0:T(8,128)(2,1)} %get-tuple-element.9) | data formatting | bytes 196608
  117.2 1.5 %copy.17 = bf16[1,64,768]{2,1,0:T(8,128)(2,1)} copy(bf16[1,64,768]{2,1,0:T(8,128)(2,1)} %get-tuple-element.10) | data formatting | bytes 196608
  118.8 1.5 %copy.18 = bf16[1,48,1024]{2,1,0:T(8,128)(2,1)} copy(bf16[1,48,1024]{2,1,0:T(8,128)(2,1)} %get-tuple-element.11) | data formatting | bytes 196608

commit v3 on v1

--- a/solution.py
+++ b/solution.py
@@ -21,16 +21,16 @@
 
 def fused(
     sizes,
-    ids_ref, logits_ref, x_ref, g_ref, wg_hbm, wu_hbm, wd_hbm,
+    ids_hbm, logits_hbm, x_hbm, g_hbm, wg_hbm, wu_hbm, wd_hbm,
     tok_ref, gate_ref, up_ref, down_ref,
-    ids_send, logits_pad, ids_all, ids_flat,
+    ids_ref, logits_ref, ids_send, logits_pad, ids_all, ids_flat,
     wg, wu, wd,
     xcat, gcat, onehot, send_x, send_g, got_x, got_g,
     xs, xs_t, dy, act_t, coef1, coef3, dh1, dh3, gates,
     dx_cat, send_r, got_r,
     part_g, part_u, part_d0, part_d1,
     ring_g, ring_u, ring_d0, ring_d1,
-    w_sem, ids_ssem, ids_rsem, fwd_ssem, fwd_rsem, own_sem, ret_ssem, ret_rsem,
+    w_sem, in_sem, ids_ssem, ids_rsem, fwd_ssem, fwd_rsem, own_sem, ret_ssem, ret_rsem,
     ring_ssem, ring_rsem,
 ):
     E, G, T, D, F, C = sizes
@@ -47,53 +47,82 @@
     z_right = lax.rem(z + 1, G)
     z_left = lax.rem(z + G - 1, G)
 
+    RW = min(8, E // 2)
+    CW = E // RW
+    row_at = me // RW
+    col_at = lax.rem(me, RW)
+
+    small = [
+        pltpu.make_async_copy(src, dst, in_sem.at[k])
+        for k, (src, dst) in enumerate(((ids_hbm, ids_ref), (logits_hbm, logits_ref)))
+    ]
+    for copy in small:
+        copy.start()
+
+    def row_mate(k):
+        return row_at * RW + lax.rem(col_at + k, RW)
+
+    def col_mate(k):
+        return lax.rem(row_at + k, CW) * RW + col_at
+
+    barrier = pltpu.get_barrier_semaphore()
+    mates = [(z, row_mate(k)) for k in range(1, RW)] + [(z, col_mate(k)) for k in range(1, CW)]
+    for other in mates + [(z_right, me), (z_left, me)]:
+        pl.semaphore_signal(barrier, inc=1, device_id=other, device_id_type=MESH)
+
+    for m in range(2):
+        for q in range(4):
+            rows = pl.ds((q * 2 + m) * T, T)
+            pltpu.make_async_copy(
+                x_hbm.at[m, :, pl.ds(q * Q, Q)], xcat.at[rows, :], in_sem.at[2]
+            ).start()
+    for copy in small:
+        copy.wait()
+
+    ids_send[...] = jnp.full(ids_send.shape, -1, jnp.int32)
+    logits_pad[...] = jnp.zeros(logits_pad.shape, jnp.int32)
+    for m in range(2):
+        ids_send[m : m + 1, 0:C] = ids_ref[m, 0]
+        logits_pad[m : m + 1, 0:C] = logits_ref[m, 0]
+    ids_all[pl.ds(me, 1)] = ids_send[...][None]
+
+    pl.semaphore_wait(barrier, RW - 1 + CW - 1 + 2)
+
+    for k in range(1, RW):
+        pltpu.make_async_remote_copy(
+            src_ref=ids_send,
+            dst_ref=ids_all.at[me],
+            send_sem=ids_ssem.at[0],
+            recv_sem=ids_rsem.at[0],
+            device_id=(z, row_mate(k)),
+            device_id_type=MESH,
+        ).start()
+    near = ids_all.at[pl.ds(0, max(RW - 1, 1))]
+    if RW > 1:
+        pltpu.make_async_copy(near, near, ids_rsem.at[0]).wait()
+    ours = ids_all.at[pl.ds(row_at * RW, RW)]
+    for k in range(1, CW):
+        pltpu.make_async_remote_copy(
+            src_ref=ours,
+            dst_ref=ours,
+            send_sem=ids_ssem.at[1],
+            recv_sem=ids_rsem.at[1],
+            device_id=(z, col_mate(k)),
+            device_id_type=MESH,
+        ).start()
+
+    for m in range(2):
+        for q in range(4):
+            rows = pl.ds((q * 2 + m) * T, T)
+            pltpu.make_async_copy(
+                g_hbm.at[m, :, pl.ds(q * Q, Q)], gcat.at[rows, :], in_sem.at[3]
+            ).start()
     weights = [
         pltpu.make_async_copy(src.at[0], dst, w_sem.at[k])
         for k, (src, dst) in enumerate(((wg_hbm, wg), (wu_hbm, wu), (wd_hbm, wd)))
     ]
     for copy in weights:
         copy.start()
-
-    barrier = pltpu.get_barrier_semaphore()
-
-    def greet(k, carry):
-        pl.semaphore_signal(
-            barrier, inc=1, device_id=(z, lax.rem(me + k, E)), device_id_type=MESH
-        )
-        return carry
-
-    lax.fori_loop(1, E, greet, 0)
-    for other in (z_right, z_left):
-        pl.semaphore_signal(barrier, inc=1, device_id=(other, me), device_id_type=MESH)
-
-    ids_send[...] = jnp.full(ids_send.shape, -1, jnp.int32)
-    logits_pad[...] = jnp.zeros(logits_pad.shape, jnp.int32)
-    for m in range(2):
-        ids_send[m : m + 1, 0:C] = ids_ref[m, 0]
-        logits_pad[m : m + 1, 0:C] = logits_ref[m, 0]
-    ids_all[pl.ds(me, 1)] = ids_send[...][None]
-
-    pl.semaphore_wait(barrier, E - 1 + 2)
-
-    def send_ids(k, carry):
-        pltpu.make_async_remote_copy(
-            src_ref=ids_send,
-            dst_ref=ids_all.at[me],
-            send_sem=ids_ssem,
-            recv_sem=ids_rsem,
-            device_id=(z, lax.rem(me + k, E)),
-            device_id_type=MESH,
-        ).start()
-        return carry
-
-    lax.fori_loop(1, E, send_ids, 0)
-
-    for m in range(2):
-        for q in range(4):
-            rows = pl.ds((q * 2 + m) * T, T)
-            xcat[rows, :] = x_ref[m, :, q * Q : (q + 1) * Q]
-            gcat[rows, :] = g_ref[m, :, q * Q : (q + 1) * Q]
-
     row = iota((R4, 128), 0)
     micro_row = (row // 2) % 2
     mine = jnp.where(micro_row == 0, ids_send[0:1, :], ids_send[1:2, :]).astype(F32)
@@ -106,7 +135,8 @@
     logit = jnp.sum(jnp.where(inside & (mine == pick), marks, 0.0), axis=1, keepdims=True)
     gates[...] = jax.nn.sigmoid(logit * (1.0 / 4096.0))
 
-    pltpu.make_async_copy(ids_all.at[pl.ds(0, E - 1)], ids_all.at[pl.ds(0, E - 1)], ids_rsem).wait()
+    rest = ids_all.at[pl.ds(0, (CW - 1) * RW)]
+    pltpu.make_async_copy(rest, rest, ids_rsem.at[1]).wait()
 
     for e in range(E):
         for m in range(2):
@@ -125,29 +155,14 @@
         table = jnp.where(lane == 2 * m + 1, last_ok, table)
     table = table.astype(BF16)
 
-    OB = min(128, E * 16)
-    for blk in range(E * 16 // OB):
-        rows = pl.ds(blk * OB, OB)
-        spread = (
-            (iota((OB, E), 0) + blk * OB) // 16 == iota((OB, E), 1)
-        ).astype(F32).astype(BF16)
-        values = jnp.dot(spread, table, preferred_element_type=F32)
-        row = iota((OB, 128), 0)
-        chosen = jnp.sum(
-            jnp.where(iota((OB, 128), 1) == row % 4, values, 0.0), axis=1, keepdims=True
-        )
-        line = iota((OB, 1), 0)
-        place = ((line // 4) % 4) * (2 * T) + ((line // 2) % 2) * T
-        target = jnp.where(chosen < 0.0, -1.0, chosen + place.astype(F32))
-        hot = (iota((OB, 8 * T), 1).astype(F32) == target).astype(F32).astype(BF16)
-        onehot[rows, :] = hot
-        send_x[rows, :] = jnp.dot(hot, xcat[...], preferred_element_type=F32).astype(BF16)
-
-    def exchange(src, dst, ssem, rsem, osem):
-        here = pl.ds(pl.multiple_of(me * 16, 16), 16)
+    here = pl.ds(pl.multiple_of(me * 16, 16), 16)
+
+    def keep(src, dst, osem):
         own = pltpu.make_async_copy(src.at[here], dst.at[here], osem)
         own.start()
-
+        return own
+
+    def exchange(src, dst, ssem, rsem):
         def one(k, carry):
             peer = lax.rem(me + k, E)
             pltpu.make_async_remote_copy(
@@ -161,20 +176,55 @@
             return carry
 
         lax.fori_loop(1, E, one, 0)
-        return own
 
     def arrived(dst, rsem, own):
         own.wait()
         whole = dst.at[pl.ds(0, (E - 1) * 16)]
         pltpu.make_async_copy(whole, whole, rsem).wait()
 
-    own_x = exchange(send_x, got_x, fwd_ssem.at[0], fwd_rsem.at[0], own_sem.at[0])
-    for blk in range(E * 16 // OB):
-        rows = pl.ds(blk * OB, OB)
+    OB = RW * 16
+    line = iota((OB, 1), 0)
+    place = (((line // 4) % 4) * (2 * T) + ((line // 2) % 2) * T).astype(F32)
+    mine_lane = iota((OB, 128), 1) == iota((OB, 128), 0) % 4
+    offsets = [sign * step for step in range(1, CW) for sign in (1, -1)][: CW - 1] + [0]
+
+    def send_row(row, src, dst, ssem, rsem, begin_at):
+        def one(k, carry):
+            peer = row * RW + lax.rem(col_at + k, RW)
+            pltpu.make_async_remote_copy(
+                src_ref=src.at[pl.ds(pl.multiple_of(peer * 16, 16), 16)],
+                dst_ref=dst.at[here],
+                send_sem=ssem,
+                recv_sem=rsem,
+                device_id=(z, peer),
+                device_id_type=MESH,
+            ).start()
+            return carry
+
+        lax.fori_loop(begin_at, RW, one, 0)
+
+    pltpu.make_async_copy(xcat, xcat, in_sem.at[2]).wait()
+    for offset in offsets:
+        row = lax.rem(row_at + offset + CW, CW)
+        rows = pl.ds(pl.multiple_of(row * OB, OB), OB)
+        spread = (line // 16 + row * RW == iota((OB, E), 1)).astype(F32).astype(BF16)
+        values = jnp.dot(spread, table, preferred_element_type=F32)
+        chosen = jnp.sum(jnp.where(mine_lane, values, 0.0), axis=1, keepdims=True)
+        target = jnp.where(chosen < 0.0, -1.0, chosen + place)
+        hot = (iota((OB, 8 * T), 1).astype(F32) == target).astype(F32).astype(BF16)
+        onehot[rows, :] = hot
+        send_x[rows, :] = jnp.dot(hot, xcat[...], preferred_element_type=F32).astype(BF16)
+        send_row(row, send_x, got_x, fwd_ssem.at[0], fwd_rsem.at[0], 0 if offset else 1)
+    own_x = keep(send_x, got_x, own_sem.at[0])
+    pltpu.make_async_copy(gcat, gcat, in_sem.at[3]).wait()
+    for offset in offsets:
+        row = lax.rem(row_at + offset + CW, CW)
+        rows = pl.ds(pl.multiple_of(row * OB, OB), OB)
         send_g[rows, :] = jnp.dot(
             onehot[rows, :], gcat[...], preferred_element_type=F32
         ).astype(BF16)
-    own_g = exchange(send_g, got_g, fwd_ssem.at[1], fwd_rsem.at[1], own_sem.at[1])
+        send_row(row, send_g, got_g, fwd_ssem.at[1], fwd_rsem.at[1], 0 if offset else 1)
+    own_g = keep(send_g, got_g, own_sem.at[1])
 
     r = iota((BR, BR), 0)
     c = iota((BR, BR), 1)
@@ -309,7 +359,8 @@
         send_r[rows, :] = jnp.dot(
             perm_t, dx_cat[rows, :], preferred_element_type=F32
         ).astype(BF16)
-    own_r = exchange(send_r, got_r, ret_ssem, ret_rsem, own_sem.at[2])
+    exchange(send_r, got_r, ret_ssem, ret_rsem)
+    own_r = keep(send_r, got_r, own_sem.at[2])
 
     def ring_step(step, carry):
         for way, p in order:
@@ -340,7 +391,9 @@
     gate_ref[0] = finish(0)
     up_ref[0] = finish(1)
 
-    pltpu.make_async_copy(ids_all.at[pl.ds(0, E - 1)], ids_all.at[pl.ds(0, E - 1)], ids_ssem).wait()
+    if RW > 1:
+        pltpu.make_async_copy(near, near, ids_ssem.at[0]).wait()
+    pltpu.make_async_copy(rest, rest, ids_ssem.at[1]).wait()
     for src, sem in ((send_x, fwd_ssem.at[0]), (send_g, fwd_ssem.at[1]), (send_r, ret_ssem)):
         whole = src.at[pl.ds(0, (E - 1) * 16)]
         pltpu.make_async_copy(whole, whole, sem).wait()
@@ -348,6 +401,18 @@
         for p in range(4):
             for step in range(starts[way][p], S):
                 ring_copy(way, p, step).wait_send()
+
+
+def settle(*refs):
+    number = len(refs) // 2
+    sems = refs[-1]
+    copies = [
+        pltpu.make_async_copy(refs[k], refs[number + k], sems.at[k]) for k in range(number)
+    ]
+    for copy in copies:
+        copy.start()
+    for copy in copies:
+        copy.wait()
 
 
 def body(activations, out_grads, chosen_ids, gate_logits, w_gate, w_up, w_down):
@@ -358,10 +423,11 @@
     C = chosen_ids.shape[-1]
     Q, S, R4, R16 = D // 4, G // 2, 4 * E, 16 * E
     vmem = pl.BlockSpec(memory_space=pltpu.VMEM)
-    anywhere = pl.BlockSpec(memory_space=pl.ANY)
+    hbm = pl.BlockSpec(memory_space=pltpu.HBM)
     V = pltpu.VMEM
     dma = pltpu.SemaphoreType.DMA
     scratch = [
+        V((2, 1, 1, C), jnp.int32), V((2, 1, 1, C), jnp.int32),
         V((2, 128), jnp.int32), V((2, 128), jnp.int32),
         V((E, 2, 128), jnp.int32), V((2, E, 128), jnp.int32),
         V((D, F), BF16), V((D, F), BF16), V((F, D), BF16),
@@ -373,11 +439,11 @@
         V((D, F), BF16), V((D, F), BF16), V((F, D // 2), BF16), V((F, D // 2), BF16),
         V((2, S, D // G, F), BF16), V((2, S, D // G, F), BF16),
         V((2, S, F // G, D // 2), BF16), V((2, S, F // G, D // 2), BF16),
-        dma((3,)), dma, dma, dma((2,)), dma((2,)), dma((3,)), dma, dma,
+        dma((3,)), dma((4,)), dma((2,)), dma((2,)), dma((2,)), dma((2,)), dma((3,)), dma, dma,
         dma((2, 4, S)), dma((2, 4, S)),
     ]
     shape = jax.ShapeDtypeStruct
-    return pl.pallas_call(
+    results = pl.pallas_call(
         functools.partial(fused, (E, G, T, D, F, C)),
         out_shape=(
             shape((2, T, D), BF16),
@@ -385,13 +451,21 @@
             shape((1, D // G, F), BF16),
             shape((1, F // G, D), BF16),
         ),
-        in_specs=[vmem, vmem, vmem, vmem, anywhere, anywhere, anywhere],
+        in_specs=[hbm] * 7,
         out_specs=(vmem, vmem, vmem, vmem),
         scratch_shapes=scratch,
         compiler_params=pltpu.CompilerParams(
-            collective_id=0, has_side_effects=True, vmem_limit_bytes=48 * 1024 * 1024
+            collective_id=0, has_side_effects=True, vmem_limit_bytes=64 * 1024 * 1024
         ),
     )(chosen_ids, gate_logits, activations, out_grads, w_gate, w_up, w_down)
+    return pl.pallas_call(
+        settle,
+        out_shape=tuple(shape(item.shape, item.dtype) for item in results),
+        in_specs=[hbm] * 4,
+        out_specs=(hbm,) * 4,
+        scratch_shapes=[dma((4,))],
+        compiler_params=pltpu.CompilerParams(vmem_limit_bytes=64 * 1024 * 1024),
+    )(*results)
 
 
 def solution(mesh):

time: 120 us -> 128 us (1.067)
  Pallas kernels: 109 us -> 127 us
  local copies, waits for them, and re-layouts: 10 us -> 0 us
    pallas_call x0 -> x1, Pallas kernels: none -> 16 us  [body(): pl.pallas_call(settle, out_shape=tuple((shape(item.shape, item.dtype) for...]
    unnamed x18 -> x0, local copies, waits for them, and re-layouts: 10 us -> none
    pallas_call x1, Pallas kernels: 109 us -> 111 us  [body(): pl.pallas_call(functools.partial(fused, (E, G, T, D, F, C)), out_shape=(s...]
where the time goes in v3:
time: 128 us
  Pallas kernels  127 us (99%)
    pallas_call x1, Pallas kernels, body(): pl.pallas_call(functools.partial(fused, (E, G, T, D, F, C)), out_shape=(s...  111 us
    pallas_call x1, Pallas kernels, body(): pl.pallas_call(settle, out_shape=tuple((shape(item.shape, item.dtype) for...  16 us

profile of v3, /device:TPU:1, one launch (start us, length us, event | category | flops | bytes accessed | tf_op | source)
XLA Modules:
  0.0 127.8 jit_solution(15728210534924775012)
XLA Ops:
  0.6 111.1 %shard_map.102 = (bf16[2,48,1024]{2,1,0:T(8,128)(2,1)}, bf16[1,64,768]{2,1,0:T(8,128)(2,1)}, bf16[1,64,768]{2,1,0:T(8,128)(2,1)}, bf16[1,48,1024]{2,1,0:T(8,128)(2,1)}) custom-call(s32[2,1,1,96]{3,2,1,0:T(1,128)} %ids_hbm.1, s32[2,1,1,96]{3,2,1,0:T(1,128)} %logits_hbm.1, bf16[2,48,1024]{2,1,0:T(8,128)(2,1)} %x_hbm.1, bf16[2,48,1024]{2,1,0:T(8,128)(2,1)} %g_hbm.1, ...), custom_call_target="tpu_custom_call" | custom-call | tf_op jit(solution)/shard_map/pallas_call | solution.py:446
  111.7 16.0 %shard_map.103 = (bf16[2,48,1024]{2,1,0:T(8,128)(2,1)}, bf16[1,64,768]{2,1,0:T(8,128)(2,1)}, bf16[1,64,768]{2,1,0:T(8,128)(2,1)}, bf16[1,48,1024]{2,1,0:T(8,128)(2,1)}) custom-call(bf16[2,48,1024]{2,1,0:T(8,128)(2,1)} %get-tuple-element.8.refs_0_, bf16[1,64,768]{2,1,0:T(8,128)(2,1)} %get-tuple-element.9.refs_1_, ...), custom_call_target="tpu_custom_call" | custom-call | tf_op jit(solution)/shard_map/pallas_call | solution.py:461

commit v4 on v3

--- a/solution.py
+++ b/solution.py
@@ -117,12 +117,6 @@
             pltpu.make_async_copy(
                 g_hbm.at[m, :, pl.ds(q * Q, Q)], gcat.at[rows, :], in_sem.at[3]
             ).start()
-    weights = [
-        pltpu.make_async_copy(src.at[0], dst, w_sem.at[k])
-        for k, (src, dst) in enumerate(((wg_hbm, wg), (wu_hbm, wu), (wd_hbm, wd)))
-    ]
-    for copy in weights:
-        copy.start()
     row = iota((R4, 128), 0)
     micro_row = (row // 2) % 2
     mine = jnp.where(micro_row == 0, ids_send[0:1, :], ids_send[1:2, :]).astype(F32)
@@ -216,6 +210,12 @@
         send_x[rows, :] = jnp.dot(hot, xcat[...], preferred_element_type=F32).astype(BF16)
         send_row(row, send_x, got_x, fwd_ssem.at[0], fwd_rsem.at[0], 0 if offset else 1)
     own_x = keep(send_x, got_x, own_sem.at[0])
+    weights = [
+        pltpu.make_async_copy(src.at[0], dst, w_sem.at[k])
+        for k, (src, dst) in enumerate(((wg_hbm, wg), (wu_hbm, wu), (wd_hbm, wd)))
+    ]
+    for copy in weights:
+        copy.start()
     pltpu.make_async_copy(gcat, gcat, in_sem.at[3]).wait()
     for offset in offsets:
         row = lax.rem(row_at + offset + CW, CW)
@@ -455,16 +455,16 @@
         out_specs=(vmem, vmem, vmem, vmem),
         scratch_shapes=scratch,
         compiler_params=pltpu.CompilerParams(
-            collective_id=0, has_side_effects=True, vmem_limit_bytes=64 * 1024 * 1024
+            collective_id=0, has_side_effects=True, vmem_limit_bytes=533 * 1024 * 1024 // 10
         ),
     )(chosen_ids, gate_logits, activations, out_grads, w_gate, w_up, w_down)
     return pl.pallas_call(
         settle,
         out_shape=tuple(shape(item.shape, item.dtype) for item in results),
-        in_specs=[hbm] * 4,
+        in_specs=[vmem] * 4,
         out_specs=(hbm,) * 4,
         scratch_shapes=[dma((4,))],
-        compiler_params=pltpu.CompilerParams(vmem_limit_bytes=64 * 1024 * 1024),
+        compiler_params=pltpu.CompilerParams(vmem_limit_bytes=16 * 1024 * 1024),
     )(*results)
 
 

time: 128 us -> 113 us (0.88)
  Pallas kernels: 127 us -> 111 us
  local copies, waits for them, and re-layouts: 0 us -> 1.35 us
    pallas_call x1, Pallas kernels: 16 us -> 0.81 us  [body(): pl.pallas_call(settle, out_shape=tuple((shape(item.shape, item.dtype) for...]
    unnamed x0 -> x4, local copies, waits for them, and re-layouts: none -> 1.35 us
where the time goes in v4:
time: 113 us
  Pallas kernels  111 us (98%)
  local copies, waits for them, and re-layouts  1.35 us (1%)
    pallas_call x1, Pallas kernels, body(): pl.pallas_call(functools.partial(fused, (E, G, T, D, F, C)), out_shape=(s...  110 us

profile of v4, /device:TPU:1, one launch (start us, length us, event | category | flops | bytes accessed | tf_op | source)
XLA Modules:
  0.0 113.1 jit_solution(17213732253359583459)
XLA Ops:
  0.6 0.0 copy-start
  0.6 0.7 copy-done
  1.3 0.0 copy-start.1
  1.3 0.7 copy-done.1
  2.0 110.3 %shard_map.102 = (bf16[2,48,1024]{2,1,0:T(8,128)(2,1)S(1)}, bf16[1,64,768]{2,1,0:T(8,128)(2,1)S(1)}, bf16[1,64,768]{2,1,0:T(8,128)(2,1)S(1)}, bf16[1,48,1024]{2,1,0:T(8,128)(2,1)S(1)}) custom-call(s32[2,1,1,96]{3,2,1,0:T(1,128)S(1)} %copy-done, s32[2,1,1,96]{3,2,1,0:T(1,128)S(1)} %copy-done.1, bf16[2,48,1024]{2,1,0:T(8,128)(2,1)} %x_hbm.1, ...), custom_call_target="tpu_custom_call" | custom-call | tf_op jit(solution)/shard_map/pallas_call | solution.py:446
  112.3 0.8 shard_map.103
Async XLA Ops:
  0.6 0.7 copy-start
  1.3 0.7 copy-start.1

commit v5 on v3

--- a/solution.py
+++ b/solution.py
@@ -123,6 +123,7 @@
     ]
     for copy in weights:
         copy.start()
+
     row = iota((R4, 128), 0)
     micro_row = (row // 2) % 2
     mine = jnp.where(micro_row == 0, ids_send[0:1, :], ids_send[1:2, :]).astype(F32)
@@ -188,9 +189,11 @@
     mine_lane = iota((OB, 128), 1) == iota((OB, 128), 0) % 4
     offsets = [sign * step for step in range(1, CW) for sign in (1, -1)][: CW - 1] + [0]
 
-    def send_row(row, src, dst, ssem, rsem, begin_at):
+    def send_row(offset, parity, src, dst, ssem, rsem):
+        row = lax.rem(row_at + offset + CW, CW)
+
         def one(k, carry):
-            peer = row * RW + lax.rem(col_at + k, RW)
+            peer = row * RW + lax.rem(col_at // 2 + k, RW // 2) * 2 + parity
             pltpu.make_async_remote_copy(
                 src_ref=src.at[pl.ds(pl.multiple_of(peer * 16, 16), 16)],
                 dst_ref=dst.at[here],
@@ -201,7 +204,8 @@
             ).start()
             return carry
 
-        lax.fori_loop(begin_at, RW, one, 0)
+        own = jnp.where(lax.rem(col_at, 2) == parity, 1, 0) if offset == 0 else 0
+        lax.fori_loop(own, RW // 2, one, 0)
 
     pltpu.make_async_copy(xcat, xcat, in_sem.at[2]).wait()
     for offset in offsets:
@@ -214,7 +218,7 @@
         hot = (iota((OB, 8 * T), 1).astype(F32) == target).astype(F32).astype(BF16)
         onehot[rows, :] = hot
         send_x[rows, :] = jnp.dot(hot, xcat[...], preferred_element_type=F32).astype(BF16)
-        send_row(row, send_x, got_x, fwd_ssem.at[0], fwd_rsem.at[0], 0 if offset else 1)
+        send_row(offset, 0, send_x, got_x, fwd_ssem.at[0], fwd_rsem.at[0])
     own_x = keep(send_x, got_x, own_sem.at[0])
     pltpu.make_async_copy(gcat, gcat, in_sem.at[3]).wait()
     for offset in offsets:
@@ -223,7 +227,11 @@
         send_g[rows, :] = jnp.dot(
             onehot[rows, :], gcat[...], preferred_element_type=F32
         ).astype(BF16)
-        send_row(row, send_g, got_g, fwd_ssem.at[1], fwd_rsem.at[1], 0 if offset else 1)
+        send_row(offset, 0, send_g, got_g, fwd_ssem.at[1], fwd_rsem.at[1])
+    for offset in offsets:
+        send_row(offset, 1, send_x, got_x, fwd_ssem.at[0], fwd_rsem.at[0])
+    for offset in offsets:
+        send_row(offset, 1, send_g, got_g, fwd_ssem.at[1], fwd_rsem.at[1])
     own_g = keep(send_g, got_g, own_sem.at[1])
 
     r = iota((BR, BR), 0)
@@ -455,16 +463,16 @@
         out_specs=(vmem, vmem, vmem, vmem),
         scratch_shapes=scratch,
         compiler_params=pltpu.CompilerParams(
-            collective_id=0, has_side_effects=True, vmem_limit_bytes=64 * 1024 * 1024
+            collective_id=0, has_side_effects=True, vmem_limit_bytes=533 * 1024 * 1024 // 10
         ),
     )(chosen_ids, gate_logits, activations, out_grads, w_gate, w_up, w_down)
     return pl.pallas_call(
         settle,
         out_shape=tuple(shape(item.shape, item.dtype) for item in results),
-        in_specs=[hbm] * 4,
+        in_specs=[vmem] * 4,
         out_specs=(hbm,) * 4,
         scratch_shapes=[dma((4,))],
-        compiler_params=pltpu.CompilerParams(vmem_limit_bytes=64 * 1024 * 1024),
+        compiler_params=pltpu.CompilerParams(vmem_limit_bytes=16 * 1024 * 1024),
     )(*results)
 
 

time: 128 us -> 108 us (0.84)
  Pallas kernels: 127 us -> 106 us
  local copies, waits for them, and re-layouts: 0 us -> 1.35 us
    pallas_call x1, Pallas kernels: 16 us -> 0.81 us  [body(): pl.pallas_call(settle, out_shape=tuple((shape(item.shape, item.dtype) for...]
    pallas_call x1, Pallas kernels: 111 us -> 105 us  [body(): pl.pallas_call(functools.partial(fused, (E, G, T, D, F, C)), out_shape=(s...]
    unnamed x0 -> x4, local copies, waits for them, and re-layouts: none -> 1.35 us
where the time goes in v5:
time: 108 us
  Pallas kernels  106 us (98%)
  local copies, waits for them, and re-layouts  1.35 us (1%)
    pallas_call x1, Pallas kernels, body(): pl.pallas_call(functools.partial(fused, (E, G, T, D, F, C)), out_shape=(s...  105 us

profile of v5, /device:TPU:1, one launch (start us, length us, event | category | flops | bytes accessed | tf_op | source)
XLA Modules:
  0.0 107.8 jit_solution(18041166138213522973)
XLA Ops:
  0.6 0.0 copy-start
  0.6 0.7 copy-done
  1.3 0.0 copy-start.1
  1.3 0.7 copy-done.1
  2.0 105.0 %shard_map.102 = (bf16[2,48,1024]{2,1,0:T(8,128)(2,1)S(1)}, bf16[1,64,768]{2,1,0:T(8,128)(2,1)S(1)}, bf16[1,64,768]{2,1,0:T(8,128)(2,1)S(1)}, bf16[1,48,1024]{2,1,0:T(8,128)(2,1)S(1)}) custom-call(s32[2,1,1,96]{3,2,1,0:T(1,128)S(1)} %copy-done, s32[2,1,1,96]{3,2,1,0:T(1,128)S(1)} %copy-done.1, bf16[2,48,1024]{2,1,0:T(8,128)(2,1)} %x_hbm.1, ...), custom_call_target="tpu_custom_call" | custom-call | tf_op jit(solution)/shard_map/pallas_call | solution.py:454
  107.0 0.8 shard_map.103
Async XLA Ops:
  0.6 0.7 copy-start
  1.3 0.7 copy-start.1

commit v6 on v5

--- a/solution.py
+++ b/solution.py
@@ -106,7 +106,7 @@
             src_ref=ours,
             dst_ref=ours,
             send_sem=ids_ssem.at[1],
-            recv_sem=ids_rsem.at[1],
+            recv_sem=ids_rsem.at[1 + row_at],
             device_id=(z, col_mate(k)),
             device_id_type=MESH,
         ).start()
@@ -137,24 +137,24 @@
     gates[...] = jax.nn.sigmoid(logit * (1.0 / 4096.0))
 
     rest = ids_all.at[pl.ds(0, (CW - 1) * RW)]
-    pltpu.make_async_copy(rest, rest, ids_rsem.at[1]).wait()
-
-    for e in range(E):
+
+    lane = iota((RW, 128), 1)
+    base = (me * T).astype(F32)
+
+    def wanted(row):
+        table = jnp.full((RW, 128), -1.0, F32)
         for m in range(2):
-            ids_flat[m, e : e + 1, :] = ids_all[e, m : m + 1, :]
-    lane = iota((E, 128), 1)
-    table = jnp.full((E, 128), -1.0, F32)
-    base = (me * T).astype(F32)
-    for m in range(2):
-        local = ids_flat[m].astype(F32) - base
-        inside = (local >= 0.0) & (local < float(T))
-        first = jnp.min(jnp.where(inside, local, 1e6), axis=1, keepdims=True)
-        last = jnp.max(jnp.where(inside, local, -1.0), axis=1, keepdims=True)
-        first_ok = jnp.where(first < 1e5, first, -1.0)
-        last_ok = jnp.where(last > first, last, -1.0)
-        table = jnp.where(lane == 2 * m, first_ok, table)
-        table = jnp.where(lane == 2 * m + 1, last_ok, table)
-    table = table.astype(BF16)
+            for i in range(RW):
+                ids_flat[m, i : i + 1, :] = ids_all[row * RW + i, m : m + 1, :]
+            local = ids_flat[m].astype(F32) - base
+            inside = (local >= 0.0) & (local < float(T))
+            first = jnp.min(jnp.where(inside, local, 1e6), axis=1, keepdims=True)
+            last = jnp.max(jnp.where(inside, local, -1.0), axis=1, keepdims=True)
+            first_ok = jnp.where(first < 1e5, first, -1.0)
+            last_ok = jnp.where(last > first, last, -1.0)
+            table = jnp.where(lane == 2 * m, first_ok, table)
+            table = jnp.where(lane == 2 * m + 1, last_ok, table)
+        return table
 
     here = pl.ds(pl.multiple_of(me * 16, 16), 16)
 
@@ -186,8 +186,10 @@
     OB = RW * 16
     line = iota((OB, 1), 0)
     place = (((line // 4) % 4) * (2 * T) + ((line // 2) % 2) * T).astype(F32)
+    spread = (line // 16 == iota((OB, RW), 1)).astype(F32)
     mine_lane = iota((OB, 128), 1) == iota((OB, 128), 0) % 4
-    offsets = [sign * step for step in range(1, CW) for sign in (1, -1)][: CW - 1] + [0]
+    offsets = [sign * step for step in range(1, CW) for sign in (1, -1)][: CW - 1]
+    offsets = [0] + offsets
 
     def send_row(offset, parity, src, dst, ssem, rsem):
         row = lax.rem(row_at + offset + CW, CW)
@@ -211,8 +213,10 @@
     for offset in offsets:
         row = lax.rem(row_at + offset + CW, CW)
         rows = pl.ds(pl.multiple_of(row * OB, OB), OB)
-        spread = (line // 16 + row * RW == iota((OB, E), 1)).astype(F32).astype(BF16)
-        values = jnp.dot(spread, table, preferred_element_type=F32)
+        if offset:
+            theirs = ids_all.at[pl.ds(row * RW, RW)]
+            pltpu.make_async_copy(theirs, theirs, ids_rsem.at[1 + row]).wait()
+        values = jnp.dot(spread, wanted(row), preferred_element_type=F32)
         chosen = jnp.sum(jnp.where(mine_lane, values, 0.0), axis=1, keepdims=True)
         target = jnp.where(chosen < 0.0, -1.0, chosen + place)
         hot = (iota((OB, 8 * T), 1).astype(F32) == target).astype(F32).astype(BF16)
@@ -430,6 +434,7 @@
     F = w_gate.shape[-1]
     C = chosen_ids.shape[-1]
     Q, S, R4, R16 = D // 4, G // 2, 4 * E, 16 * E
+    RW = min(8, E // 2)
     vmem = pl.BlockSpec(memory_space=pltpu.VMEM)
     hbm = pl.BlockSpec(memory_space=pltpu.HBM)
     V = pltpu.VMEM
@@ -437,7 +442,7 @@
     scratch = [
         V((2, 1, 1, C), jnp.int32), V((2, 1, 1, C), jnp.int32),
         V((2, 128), jnp.int32), V((2, 128), jnp.int32),
-        V((E, 2, 128), jnp.int32), V((2, E, 128), jnp.int32),
+        V((E, 2, 128), jnp.int32), V((2, RW, 128), jnp.int32),
         V((D, F), BF16), V((D, F), BF16), V((F, D), BF16),
         V((8 * T, Q), BF16), V((8 * T, Q), BF16), V((R16, 8 * T), BF16),
         V((R16, Q), BF16), V((R16, Q), BF16), V((R16, Q), BF16), V((R16, Q), BF16),
@@ -447,7 +452,7 @@
         V((D, F), BF16), V((D, F), BF16), V((F, D // 2), BF16), V((F, D // 2), BF16),
         V((2, S, D // G, F), BF16), V((2, S, D // G, F), BF16),
         V((2, S, F // G, D // 2), BF16), V((2, S, F // G, D // 2), BF16),
-        dma((3,)), dma((4,)), dma((2,)), dma((2,)), dma((2,)), dma((2,)), dma((3,)), dma, dma,
+        dma((3,)), dma((4,)), dma((2,)), dma((1 + E // RW,)), dma((2,)), dma((2,)), dma((3,)), dma, dma,
         dma((2, 4, S)), dma((2, 4, S)),
     ]
     shape = jax.ShapeDtypeStruct

time: 108 us -> 105 us (0.972)
  Pallas kernels: 106 us -> 102 us
    pallas_call x1, Pallas kernels: 105 us -> 101 us  [body(): pl.pallas_call(functools.partial(fused, (E, G, T, D, F, C)), out_shape=(s...]
where the time goes in v6:
time: 105 us; the launch traced here: 104 us
  Pallas kernels  102 us (97%)
  local copies, waits for them, and re-layouts  1.35 us (1%)
    pallas_call x1, Pallas kernels, body(): pl.pallas_call(functools.partial(fused, (E, G, T, D, F, C)), out_shape=(s...  101 us

profile of v6, /device:TPU:1, one launch (start us, length us, event | category | flops | bytes accessed | tf_op | source)
XLA Modules:
  0.0 104.1 jit_solution(4548662329415035464)
XLA Ops:
  0.6 0.0 copy-start
  0.6 0.7 copy-done
  1.3 0.0 copy-start.1
  1.3 0.7 copy-done.1
  2.0 101.3 %shard_map.102 = (bf16[2,48,1024]{2,1,0:T(8,128)(2,1)S(1)}, bf16[1,64,768]{2,1,0:T(8,128)(2,1)S(1)}, bf16[1,64,768]{2,1,0:T(8,128)(2,1)S(1)}, bf16[1,48,1024]{2,1,0:T(8,128)(2,1)S(1)}) custom-call(s32[2,1,1,96]{3,2,1,0:T(1,128)S(1)} %copy-done, s32[2,1,1,96]{3,2,1,0:T(1,128)S(1)} %copy-done.1, bf16[2,48,1024]{2,1,0:T(8,128)(2,1)} %x_hbm.1, ...), custom_call_target="tpu_custom_call" | custom-call | tf_op jit(solution)/shard_map/pallas_call | solution.py:459
  103.3 0.8 shard_map.103
Async XLA Ops:
  0.6 0.7 copy-start
  1.3 0.7 copy-start.1

commit v7 on v6

--- a/solution.py
+++ b/solution.py
@@ -163,7 +163,7 @@
         own.start()
         return own
 
-    def exchange(src, dst, ssem, rsem):
+    def exchange(src, dst, ssem, rsem, begin_at, end_at):
         def one(k, carry):
             peer = lax.rem(me + k, E)
             pltpu.make_async_remote_copy(
@@ -176,7 +176,7 @@
             ).start()
             return carry
 
-        lax.fori_loop(1, E, one, 0)
+        lax.fori_loop(begin_at, end_at, one, 0)
 
     def arrived(dst, rsem, own):
         own.wait()
@@ -371,12 +371,17 @@
         send_r[rows, :] = jnp.dot(
             perm_t, dx_cat[rows, :], preferred_element_type=F32
         ).astype(BF16)
-    exchange(send_r, got_r, ret_ssem, ret_rsem)
+    turns = max(S - 4, 1)
+    per = -(-(E - 1) // turns)
+    exchange(send_r, got_r, ret_ssem, ret_rsem, 1, min(1 + per, E))
     own_r = keep(send_r, got_r, own_sem.at[2])
 
     def ring_step(step, carry):
         for way, p in order:
             pass_on(way, p, step)
+        begin_at = jnp.minimum(1 + (step - 1) * per, E)
+        end_at = jnp.minimum(begin_at + per, E)
+        exchange(send_r, got_r, ret_ssem, ret_rsem, begin_at, end_at)
         return carry
 
     lax.fori_loop(2, S, ring_step, 0)

time: 105 us -> 105 us (level)
  no operation moved by 1% of the time
where the time goes in v7:
time: 105 us; the launch traced here: 104 us
  Pallas kernels  102 us (97%)
  local copies, waits for them, and re-layouts  1.35 us (1%)
    pallas_call x1, Pallas kernels, body(): pl.pallas_call(functools.partial(fused, (E, G, T, D, F, C)), out_shape=(s...  101 us

profile of v7, /device:TPU:1, one launch (start us, length us, event | category | flops | bytes accessed | tf_op | source)
XLA Modules:
  0.0 104.1 jit_solution(14971048824320851889)
XLA Ops:
  0.6 0.0 copy-start
  0.6 0.7 copy-done
  1.3 0.0 copy-start.1
  1.3 0.7 copy-done.1
  2.0 101.3 %shard_map.102 = (bf16[2,48,1024]{2,1,0:T(8,128)(2,1)S(1)}, bf16[1,64,768]{2,1,0:T(8,128)(2,1)S(1)}, bf16[1,64,768]{2,1,0:T(8,128)(2,1)S(1)}, bf16[1,48,1024]{2,1,0:T(8,128)(2,1)S(1)}) custom-call(s32[2,1,1,96]{3,2,1,0:T(1,128)S(1)} %copy-done, s32[2,1,1,96]{3,2,1,0:T(1,128)S(1)} %copy-done.1, bf16[2,48,1024]{2,1,0:T(8,128)(2,1)} %x_hbm.1, ...), custom_call_target="tpu_custom_call" | custom-call | tf_op jit(solution)/shard_map/pallas_call | solution.py:464
  103.3 0.8 shard_map.103
Async XLA Ops:
  0.6 0.7 copy-start
  1.3 0.7 copy-start.1
